TPU v7x, 32 devices: a whole 2x2x4 slice. The times are simulated.
32 devices in a mesh: dp: 8 (over z, x), row: 2 (over core), col: 2 (over y).
Axes of the slice: x: 2, y: 2, z: 4, core: 2. Of those that a mesh axis runs over, the one named last changes fastest.
Arguments:
- tokens: bfloat16 [16384, 768], P(('dp', 'row'), 'col'), may hold values from -6 to 6
- segments: int32 [16384], P('dp'), may hold values from 0 to 7, as said below
- positions: int32 [16384], P('dp'), may hold values from 0 to 2047, as said below
- w_qkv: bfloat16 [768, 2304], P('col', 'row'), may hold values from -0.21875 to 0.21875
- b_qkv: float32 [2304], P('row'), may hold values from -4 to 4
- w_dense: bfloat16 [768, 768], P('row', 'col'), may hold values from -1.25 to 1.25
- b_dense: float32 [768], P('col'), may hold values from -4 to 4
- w_in: bfloat16 [768, 3072], P('col', 'row'), may hold values from -0.21875 to 0.21875
- b_in: float32 [3072], P('row'), may hold values from -4 to 4
- w_out: bfloat16 [3072, 768], P('row', 'col'), may hold values from -0.109375 to 0.109375
- b_out: float32 [768], P('col'), may hold values from -4 to 4
- gain_one: float32 [768], P('col'), may hold values from 0.5 to 1.5
- shift_one: float32 [768], P('col'), may hold values from -4 to 4
- gain_two: float32 [768], P('col'), may hold values from 0.5 to 1.5
- shift_two: float32 [768], P('col'), may hold values from -4 to 4
- cotangent: bfloat16 [16384, 768], P(('dp', 'row'), 'col'), may hold values from -6 to 6
Outputs:
- mixed: float32 [16384, 768], P(('dp', 'row'), 'col')
- d_tokens: float32 [16384, 768], P(('dp', 'row'), 'col')
- d_w_qkv: float32 [768, 2304], P('col', 'row')
- d_b_qkv: float32 [2304], P('row')
- d_w_dense: float32 [768, 768], P('row', 'col')
- d_b_dense: float32 [768], P('col')
- d_w_in: float32 [768, 3072], P('col', 'row')
- d_b_in: float32 [3072], P('row')
- d_w_out: float32 [3072, 768], P('row', 'col')
- d_b_out: float32 [768], P('col')
- d_gain_one: float32 [768], P('col')
- d_shift_one: float32 [768], P('col')
- d_gain_two: float32 [768], P('col')
- d_shift_two: float32 [768], P('col')
Inputs may be any that keep to these rules, and one draw needn't show every extreme that they name: `segments`: within each pack of 2048 tokens, document numbers start at 0, never fall, and rise by one at each of exactly 7 places, so each pack holds 8 documents. The document that holds position 1024 of a pack begins 2048/16 or more positions before it and ends 2048/16 or more positions after it. Within a document, positions rise by one from token to token; every document of a pack but its first starts at 0; the first ends at position 2047.
All inputs are finite; a program needn't handle non-finite values.
Results may differ from a plain program's by a relative error of at most 0.0094.
Values may be sent and summed in bfloat16 or wider, within the bound.
A program may use at most 192 MiB of HBM per device.

v0:
```python
import jax
import jax.numpy as jnp
from jax import lax
from jax.sharding import PartitionSpec as P

HEAD_DIM = 64
ROT = 16


norm_epsilon = 1e-05
masked_fill = -1e30


def rotary_tables(position):
    steps = jnp.arange(ROT // 2, dtype=jnp.int32).astype(jnp.float32)
    inverse = 10000.0 ** (-2.0 * steps / ROT)
    angle = position.astype(jnp.float32)[:, None] * inverse[None, :]
    angle = jnp.concatenate([angle, angle], axis=1)
    return (jnp.cos(angle), jnp.sin(angle))


def rotary(part, cosines, sines):
    turned = part[..., :ROT]
    swapped = jnp.concatenate([-turned[..., ROT // 2 :], turned[..., : ROT // 2]], axis=-1)
    rotated = turned * cosines[:, None, :] + swapped * sines[:, None, :]
    return jnp.concatenate([rotated, part[..., ROT:]], axis=-1)


def rotary_back(grads, cosines, sines):
    turned = grads[..., :ROT]
    scaled = turned * sines[:, None, :]
    swapped = jnp.concatenate([scaled[..., ROT // 2 :], -scaled[..., : ROT // 2]], axis=-1)
    return jnp.concatenate([turned * cosines[:, None, :] + swapped, grads[..., ROT:]], axis=-1)


def gelu_exact(values):
    return jax.nn.gelu(values, approximate=False)


def block_layout(query_heads):
    head_count, query_rows, depth = query_heads.shape
    block = min(512, query_rows)
    per_head = query_rows // block
    total = head_count * per_head
    numbers = jnp.arange(total, dtype=jnp.int32)
    return (block, per_head, numbers // per_head, numbers % per_head)


def block_scores(
    query_block, keys_here, query_segments, key_segments, query_start, block_id, block
):
    begin_row = block_id * block
    segs_here = lax.dynamic_slice_in_dim(query_segments, begin_row, block)
    places = query_start + begin_row + jnp.arange(block, dtype=jnp.int32)
    key_places = jnp.arange(keys_here.shape[0], dtype=jnp.int32)
    allowed = (segs_here[:, None] == key_segments[None, :]) & (
        places[:, None] >= key_places[None, :]
    )
    raw = lax.dot_general(
        query_block, keys_here, (((1,), (1,)), ((), ())), preferred_element_type=jnp.float32
    ) * HEAD_DIM ** (-0.5)
    return jnp.where(allowed, raw, masked_fill)


def attend_forward(query_heads, key_heads, value_heads, query_segments, key_segments, query_start):
    head_count, query_rows, depth = query_heads.shape
    block, per_head, head_ids, block_ids = block_layout(query_heads)
    query_blocks = query_heads.reshape(head_count * per_head, block, depth)

    def one_block(element):
        query_block, head_id, block_id = element
        keys_here = lax.dynamic_index_in_dim(key_heads, head_id, 0, keepdims=False)
        values_here = lax.dynamic_index_in_dim(value_heads, head_id, 0, keepdims=False)
        masked = block_scores(
            query_block, keys_here, query_segments, key_segments, query_start, block_id, block
        )
        highest = jnp.max(masked, axis=1, keepdims=True)
        lifted = jnp.exp(masked - highest)
        totals = jnp.sum(lifted, axis=1, keepdims=True)
        soft = (lifted / totals).astype(jnp.bfloat16)
        context = jnp.dot(soft, values_here, preferred_element_type=jnp.float32)
        return (context.astype(jnp.bfloat16), (highest + jnp.log(totals))[:, 0])

    contexts, log_totals = lax.map(one_block, (query_blocks, head_ids, block_ids))
    return (
        contexts.reshape(head_count, query_rows, depth),
        log_totals.reshape(head_count, query_rows),
    )


def attend_backward(
    query_heads,
    key_heads,
    value_heads,
    grad_heads,
    log_totals,
    query_segments,
    key_segments,
    query_start,
):
    head_count, query_rows, depth = query_heads.shape
    block, per_head, head_ids, block_ids = block_layout(query_heads)
    total = head_count * per_head
    elements = (
        query_heads.reshape(total, block, depth),
        grad_heads.reshape(total, block, depth),
        log_totals.reshape(total, block),
        head_ids,
        block_ids,
    )

    def one_block(running, element):
        key_grads, value_grads = running
        query_block, grad_block, lse_block, head_id, block_id = element
        keys_here = lax.dynamic_index_in_dim(key_heads, head_id, 0, keepdims=False)
        values_here = lax.dynamic_index_in_dim(value_heads, head_id, 0, keepdims=False)
        masked = block_scores(
            query_block, keys_here, query_segments, key_segments, query_start, block_id, block
        )
        soft = jnp.exp(masked - lse_block[:, None])
        grad_soft = lax.dot_general(
            grad_block, values_here, (((1,), (1,)), ((), ())), preferred_element_type=jnp.float32
        )
        inner = jnp.sum(soft * grad_soft, axis=1, keepdims=True)
        grad_raw = (soft * (grad_soft - inner)).astype(jnp.bfloat16)
        query_grad = jnp.dot(
            grad_raw, keys_here, preferred_element_type=jnp.float32
        ) * HEAD_DIM ** (-0.5)
        key_part = lax.dot_general(
            grad_raw, query_block, (((0,), (0,)), ((), ())), preferred_element_type=jnp.float32
        ) * HEAD_DIM ** (-0.5)
        value_part = lax.dot_general(
            soft.astype(jnp.bfloat16),
            grad_block,
            (((0,), (0,)), ((), ())),
            preferred_element_type=jnp.float32,
        )
        key_grads = key_grads.at[head_id].add(key_part)
        value_grads = value_grads.at[head_id].add(value_part)
        return ((key_grads, value_grads), query_grad)

    zeros_like_keys = jnp.zeros(key_heads.shape, jnp.float32)
    (key_grads, value_grads), query_grads = lax.scan(
        one_block, (zeros_like_keys, zeros_like_keys), elements
    )
    return (query_grads.reshape(head_count, query_rows, depth), key_grads, value_grads)


def body(
    tokens,
    segments,
    positions,
    w_qkv,
    b_qkv,
    w_dense,
    b_dense,
    w_in,
    b_in,
    w_out,
    b_out,
    gain_one,
    shift_one,
    gain_two,
    shift_two,
    cotangent,
):
    rows_here, width = tokens.shape
    col_size = lax.axis_size("col")
    features = width * col_size
    length = segments.shape[0]
    qkv_here = w_qkv.shape[1]
    hidden_here = w_in.shape[1]
    inputs = tokens.astype(jnp.float32)
    moments = lax.psum((jnp.sum(inputs, axis=1), jnp.sum(inputs * inputs, axis=1)), "col")
    average = moments[0] / features
    spread = moments[1] / features - average * average
    inv_std = lax.rsqrt(spread + norm_epsilon)
    normed = (inputs - average[:, None]) * inv_std[:, None]
    first_in = (normed * gain_one + shift_one).astype(jnp.bfloat16)
    second_in = (normed * gain_two + shift_two).astype(jnp.bfloat16)
    first_all, second_all = (
        lax.all_gather(first_in, "row", axis=0, tiled=True),
        lax.all_gather(second_in, "row", axis=0, tiled=True),
    )
    block_count = 1
    query_rows = length // col_size
    query_start = lax.axis_index("col") * query_rows
    own_block = 0
    qkv_width = qkv_here // block_count
    hidden_width = hidden_here // block_count
    qkv_blocks = w_qkv.reshape(width, block_count, qkv_width)
    in_blocks = w_in.reshape(width, block_count, hidden_width)
    summed = lax.psum_scatter(
        jnp.concatenate(
            [
                jnp.dot(first_all, w_qkv, preferred_element_type=jnp.float32),
                jnp.dot(second_all, w_in, preferred_element_type=jnp.float32),
            ],
            axis=1,
        ),
        "col",
        scatter_dimension=0,
        tiled=True,
    )
    qkv_bias = lax.dynamic_index_in_dim(
        b_qkv.reshape(block_count, qkv_width), own_block, 0, keepdims=False
    )
    in_bias = lax.dynamic_index_in_dim(
        b_in.reshape(block_count, hidden_width), own_block, 0, keepdims=False
    )
    joined_qkv = (summed[:, :qkv_width] + qkv_bias).reshape(query_rows, -1, 3, HEAD_DIM)
    hidden = summed[:, qkv_width:] + in_bias
    active = gelu_exact(hidden).astype(jnp.bfloat16)
    query_segments = lax.dynamic_slice_in_dim(segments, query_start, query_rows)
    query_positions = lax.dynamic_slice_in_dim(positions, query_start, query_rows)
    cosines, sines = rotary_tables(query_positions)
    query_heads = jnp.transpose(
        rotary(joined_qkv[:, :, 0], cosines, sines).astype(jnp.bfloat16), (1, 0, 2)
    )
    key_heads = jnp.transpose(
        rotary(joined_qkv[:, :, 1], cosines, sines).astype(jnp.bfloat16), (1, 0, 2)
    )
    value_heads = jnp.transpose(joined_qkv[:, :, 2].astype(jnp.bfloat16), (1, 0, 2))
    key_heads, value_heads = (
        lax.all_gather(key_heads, "col", axis=1, tiled=True),
        lax.all_gather(value_heads, "col", axis=1, tiled=True),
    )
    contexts, log_totals = attend_forward(
        query_heads, key_heads, value_heads, query_segments, segments, query_start
    )
    context_rows = jnp.transpose(contexts, (1, 0, 2)).reshape(query_rows, -1)
    context_parts, active_parts = (
        lax.all_gather(context_rows[None], "col", axis=0, tiled=True),
        lax.all_gather(active[None], "col", axis=0, tiled=True),
    )
    context_blocks = context_parts.reshape(block_count, length, -1)
    active_blocks = active_parts.reshape(block_count, length, -1)
    dense_blocks = w_dense.reshape(block_count, -1, w_dense.shape[1])
    out_blocks = w_out.reshape(block_count, -1, w_out.shape[1])
    branches = lax.psum_scatter(
        jnp.einsum("btj,bjo->to", context_blocks, dense_blocks, preferred_element_type=jnp.float32)
        + jnp.einsum("btf,bfo->to", active_blocks, out_blocks, preferred_element_type=jnp.float32),
        "row",
        scatter_dimension=0,
        tiled=True,
    )
    mixed = inputs + branches + b_dense + b_out
    grad_all = lax.all_gather(cotangent, "row", axis=0, tiled=True)
    d_dense = jnp.einsum(
        "btj,to->bjo", context_blocks, grad_all, preferred_element_type=jnp.float32
    ).reshape(w_dense.shape)
    d_out = jnp.einsum(
        "btf,to->bfo", active_blocks, grad_all, preferred_element_type=jnp.float32
    ).reshape(w_out.shape)
    d_out_bias = jnp.sum(grad_all, axis=0, dtype=jnp.float32)
    stacked = jnp.concatenate([dense_blocks, out_blocks], axis=1)
    back_sums = lax.psum_scatter(
        jnp.einsum("to,bjo->tbj", grad_all, stacked, preferred_element_type=jnp.float32),
        "col",
        scatter_dimension=0,
        tiled=True,
    )
    back_sums = back_sums.reshape(query_rows, -1)
    context_width = dense_blocks.shape[1]
    context_grad = back_sums[:, :context_width].astype(jnp.bfloat16)
    active_grad = back_sums[:, context_width:]
    hidden_grad = jax.vjp(gelu_exact, hidden)[1](active_grad)[0].astype(jnp.bfloat16)
    grad_heads = jnp.transpose(context_grad.reshape(query_rows, -1, HEAD_DIM), (1, 0, 2))
    query_grads, key_grads, value_grads = attend_backward(
        query_heads,
        key_heads,
        value_heads,
        grad_heads,
        log_totals,
        query_segments,
        segments,
        query_start,
    )
    key_grads, value_grads = (
        lax.psum_scatter(key_grads, "col", scatter_dimension=1, tiled=True),
        lax.psum_scatter(value_grads, "col", scatter_dimension=1, tiled=True),
    )
    query_back = rotary_back(jnp.transpose(query_grads, (1, 0, 2)), cosines, sines)
    key_back = rotary_back(jnp.transpose(key_grads, (1, 0, 2)), cosines, sines)
    value_back = jnp.transpose(value_grads, (1, 0, 2))
    joined_grad = (
        jnp.stack([query_back, key_back, value_back], axis=2)
        .reshape(query_rows, -1)
        .astype(jnp.bfloat16)
    )
    qkv_parts, hidden_parts = (
        lax.all_gather(joined_grad[None], "col", axis=0, tiled=True),
        lax.all_gather(hidden_grad[None], "col", axis=0, tiled=True),
    )
    qkv_grad_blocks = qkv_parts.reshape(block_count, length, -1)
    hidden_grad_blocks = hidden_parts.reshape(block_count, length, -1)
    d_qkv = jnp.einsum(
        "td,btf->dbf", first_all, qkv_grad_blocks, preferred_element_type=jnp.float32
    ).reshape(w_qkv.shape)
    d_qkv_bias = jnp.sum(qkv_grad_blocks, axis=1, dtype=jnp.float32).reshape(-1)
    d_in = jnp.einsum(
        "td,btf->dbf", second_all, hidden_grad_blocks, preferred_element_type=jnp.float32
    ).reshape(w_in.shape)
    d_in_bias = jnp.sum(hidden_grad_blocks, axis=1, dtype=jnp.float32).reshape(-1)
    norm_grads = lax.psum_scatter(
        jnp.concatenate(
            [
                jnp.einsum(
                    "btf,dbf->td", qkv_grad_blocks, qkv_blocks, preferred_element_type=jnp.float32
                ),
                jnp.einsum(
                    "btf,dbf->td", hidden_grad_blocks, in_blocks, preferred_element_type=jnp.float32
                ),
            ],
            axis=1,
        ),
        "row",
        scatter_dimension=0,
        tiled=True,
    )
    first_grad = norm_grads[:, :width]
    second_grad = norm_grads[:, width:]
    hat_grad = first_grad * gain_one + second_grad * gain_two
    hat_sums = lax.psum((jnp.sum(hat_grad, axis=1), jnp.sum(hat_grad * normed, axis=1)), "col")
    d_tokens = cotangent.astype(jnp.float32) + inv_std[:, None] * (
        hat_grad - hat_sums[0][:, None] / features - normed * (hat_sums[1][:, None] / features)
    )
    vectors = lax.psum(
        (
            jnp.sum(first_grad * normed, axis=0),
            jnp.sum(first_grad, axis=0),
            jnp.sum(second_grad * normed, axis=0),
            jnp.sum(second_grad, axis=0),
        ),
        ("dp", "row"),
    )
    summed_grads = lax.psum((d_qkv, d_qkv_bias, d_dense, d_out_bias, d_in, d_in_bias, d_out), "dp")
    return (
        mixed,
        d_tokens,
        summed_grads[0],
        summed_grads[1],
        summed_grads[2],
        summed_grads[3],
        summed_grads[4],
        summed_grads[5],
        summed_grads[6],
        summed_grads[3],
        vectors[0],
        vectors[1],
        vectors[2],
        vectors[3],
    )


def solution(mesh):
    in_specs = (
        P(("dp", "row"), "col"),
        P("dp"),
        P("dp"),
        P("col", "row"),
        P("row"),
        P("row", "col"),
        P("col"),
        P("col", "row"),
        P("row"),
        P("row", "col"),
        P("col"),
        P("col"),
        P("col"),
        P("col"),
        P("col"),
        P(("dp", "row"), "col"),
    )
    out_specs = (
        P(("dp", "row"), "col"),
        P(("dp", "row"), "col"),
        P("col", "row"),
        P("row"),
        P("row", "col"),
        P("col"),
        P("col", "row"),
        P("row"),
        P("row", "col"),
        P("col"),
        P("col"),
        P("col"),
        P("col"),
        P("col"),
    )
    return jax.shard_map(body, mesh=mesh, in_specs=in_specs, out_specs=out_specs, check_vma=False)
```

profile of v0, /device:TPU:0, one launch (start us, length us, event | category | flops | bytes accessed | tf_op | source)
XLA Modules:
  0.0 1695.5 jit_solution(4130683566150016034)
XLA Ops:
  8.8 5.9 all-reduce.4
  19.7 10.2 all-gather.14.cloned.1.call-done
  29.9 7.8 fusion.88
  48.1 11.2 pad_maximum_fusion
  60.6 9.7 convolution_bitcast_fusion.1
  71.2 234.9 %reduce-scatter.7.cloned.1.call-done = f32[1024,2688]{0,1:T(8,128)} async-done(((f32[2048,2688]{0,1:T(8,128)}), f32[1024,2688]{0,1:T(8,128)}) %reduce-scatter.7.cloned.1.call-update) | async-done | bytes 11010064 | tf_op jit(solution)/shard_map/reduce_scatter | solution.py:193
  316.6 170.1 %reduce-scatter.11.cloned.1.call-done = f32[1024,1,1920]{0,2,1:T(8,128)} async-done(((f32[2048,1,1920]{0,2,1:T(8,128)}), f32[1024,1,1920]{0,2,1:T(8,128)}) %reduce-scatter.11.cloned.1.call-update) | async-done | bytes 7864336 | tf_op jit(solution)/shard_map/reduce_scatter | solution.py:257
  493.5 22.4 %all-gather.16.cloned.1.call-done = bf16[6,2048,64]{1,2,0:T(8,128)(2,1)} async-done(((bf16[6,1024,64]{1,2,0:T(8,128)(2,1)}), bf16[6,2048,64]{1,2,0:T(8,128)(2,1)}) %all-gather.16.cloned.1.call-update) | async-done | bytes 1572880 | tf_op jit(solution)/shard_map/all_gather | solution.py:225
  520.0 24.7 %all-gather.18.cloned.1.call-done = bf16[6,2048,64]{1,2,0:T(8,128)(2,1)} async-done(((bf16[6,1024,64]{1,2,0:T(8,128)(2,1)}), bf16[6,2048,64]{1,2,0:T(8,128)(2,1)}) %all-gather.18.cloned.1.call-update) | async-done | bytes 1572880 | tf_op jit(solution)/shard_map/all_gather | solution.py:226
  548.8 169.2 %while.28 = (s32[]{:T(128)}, bf16[12,512,64]{1,2,0:T(8,128)(2,1)}, f32[12,512]{1,0:T(8,128)}, s32[12]{0:T(128)S(1)}, s32[1024]{0:T(1024)S(1)}, /*index=5*/s32[20...) while((s32[]{:T(128)}, bf16[12,512,64]{1,2,0:T(8,128)(2,1)}, ...), condition=%wide.region_8.9_spmd, body=%wide.region_5.8_spmd.sunk | while | flops 280002560 | bytes 30645560 | solution.py:84
  722.2 337.9 %while.29 = (s32[]{:T(128)}, f32[6,2048,64]{1,2,0:T(8,128)}, f32[6,2048,64]{1,2,0:T(8,128)}, f32[12,512,64]{1,0,2:T(8,128)}, s32[12]{0:T(128)S(1)}, /*index=5*/s...) while((s32[]{:T(128)}, f32[6,2048,64]{1,2,0:T(8,128)}, ...), condition=%wide.region_14.15_spmd, body=%wide.region_11.14_spmd.sunk | while | flops 684359680 | bytes 69896080 | solution.py:143
  1060.9 17.9 %add_convert_fusion = (bf16[1024,1536]{0,1:T(8,128)(2,1)}, f32[1024,1536]{0,1:T(8,128)S(1)}) fusion(f32[1024,1920]{0,1:T(8,128)} %bitcast.188, f32[1024,2688]{0,1:T(8,128)} %reduce-scatter.7.cloned.1.call-done, f32[1536]{0:T(1024)S(1)} %copy-done.29), kind=kLoop, calls=%fused_computation.68 | loop fusion | flops 114819072 | bytes 22026240 | tf_op jit(solution)/shard_map/convert_element_type | solution.py:267
  1091.7 11.9 reduce-scatter.13.cloned.1.call-done
  1107.7 41.6 %reduce-scatter.15.cloned.1.call-done = f32[6,1024,64]{1,2,0:T(8,128)} async-done(((f32[6,2048,64]{1,2,0:T(8,128)}), f32[6,1024,64]{1,2,0:T(8,128)}) %reduce-scatter.15.cloned.1.call-update) | async-done | bytes 1572880 | tf_op jit(solution)/shard_map/reduce_scatter | solution.py:281
  1153.9 77.3 %all-gather.26.cloned.1.call-done = bf16[2048,1536]{0,1:T(8,128)(2,1)} async-done(((bf16[1024,1536]{0,1:T(8,128)(2,1)}), bf16[2048,1536]{0,1:T(8,128)(2,1)}) %all-gather.26.cloned.1.call-update) | async-done | bytes 6291472 | tf_op jit(solution)/shard_map/all_gather | solution.py:234
  1231.1 8.3 fusion.89
  1239.5 21.1 %all-gather.20.cloned.1.call-done = bf16[2,1024,384]{2,1,0:T(8,128)(2,1)} async-done(((bf16[1,1024,384]{2,1,0:T(8,128)(2,1)}), bf16[2,1024,384]{2,1,0:T(8,128)(2,1)}) %all-gather.20.cloned.1.call-update) | async-done | bytes 1572880 | tf_op jit(solution)/shard_map/all_gather | solution.py:233
  1265.8 76.5 %all-gather.28.cloned.1.call-done = bf16[2048,1536]{0,1:T(8,128)(2,1)} async-done(((bf16[1024,1536]{0,1:T(8,128)(2,1)}), bf16[2048,1536]{0,1:T(8,128)(2,1)}) %all-gather.28.cloned.1.call-update) | async-done | bytes 6291472 | tf_op jit(solution)/shard_map/all_gather | solution.py:293
  1342.3 7.9 fusion.91
  1350.2 56.9 %all-gather.24.cloned.1.call-done = bf16[2,1024,1152]{2,1,0:T(8,128)(2,1)} async-done(((bf16[1,1024,1152]{2,1,0:T(8,128)(2,1)}), bf16[2,1024,1152]{2,1,0:T(8,128)(2,1)}) %all-gather.24.cloned.1.call-update) | async-done | bytes 4718608 | tf_op jit(solution)/shard_map/all_gather | solution.py:292
  1420.4 7.8 fusion.95
  1443.2 39.4 %all-reduce.1 = (f32[1152]{0:T(1024)}, f32[384]{0:T(512)}, f32[1536]{0:T(1024)}) all-reduce(f32[1152]{0:T(1024)S(1)} %convert_reduce_fusion.1, f32[384]{0:T(512)S(1)} %convert_reduce_fusion.2, f32[1536]{0:T(1024)S(1)} %convert_reduce_fusion), channel_id=1, replica_groups=mesh['dp'=8,'row'=2,'col'=2] {'dp'}, use_global_device_ids=true, to_apply=%region_24.25 | all-reduce | flops 3072 | bytes 24576 | tf_op jit(solution)/shard_map/psum | solution.py:337
  1487.3 33.1 %all-reduce = (f32[384]{0:T(512)}, f32[384]{0:T(512)}, f32[384]{0:T(512)}, f32[384]{0:T(512)}) all-reduce(f32[384]{0:T(512)} %get-tuple-element.304, f32[384]{0:T(512)} %get-tuple-element.303, f32[384]{0:T(512)} %get-tuple-element.305, f32[384]{0:T(512)} %get-tuple-element.302), channel_id=1, replica_groups=mesh['dp'=8,'row'=2,'col'=2] {'dp','row'}, use_global_device_ids=true, to_apply=%region_33.34 | all-reduce | flops 1536 | bytes 12288 | tf_op jit(solution)/shard_map/psum | solution.py:328
  1530.1 151.4 %all-reduce.7.cloned.1.call-done = (f32[384,1152]{1,0:T(8,128)}, f32[384,384]{1,0:T(8,128)}, f32[384,1536]{1,0:T(8,128)}, f32[1536,384]{1,0:T(8,128)}) async-done(((f32[384,1152]{1,0:T(8,128)}, f32[384,384]{1,0:T(8,128)}, f32[384,1536]{1,0:T(8,128)}, f32[1536,384]{1,0:T(8,128)}), (f32[384,1152]{1,0:T(8,128)}, f32[384,384]{1,0:T(8,128)}, f32[384,1536]{1,0:T(8,128)}, ...) | async-done | bytes 7077904 | tf_op jit(solution)/shard_map/psum | solution.py:337
  (527 shorter events, 569.6 us)
Async XLA Ops:
  7.2 22.7 %all-gather.14.cloned.1.call-start = ((), (), s32[]{:S(2)}) async-start(), calls=%async_computation.7 | async-start | bytes 2359296 | tf_op jit(solution)/shard_map/all_gather | solution.py:183
  18.2 24.9 %all-gather.12.cloned.1.call-start = ((), (), s32[]{:S(2)}) async-start(), calls=%async_computation.6 | async-start | bytes 2359296 | tf_op jit(solution)/shard_map/all_gather | solution.py:182
  18.9 40.4 %all-gather.22.cloned.1.call-start = ((), (), s32[]{:S(2)}) async-start(), calls=%async_computation.13 | async-start | bytes 2359296 | tf_op jit(solution)/shard_map/all_gather | solution.py:248
  19.7 286.4 %reduce-scatter.7.cloned.1.call-start = ((), (), s32[]{:S(2)}) async-start(), calls=%async_computation.8 | async-start | bytes 33030144 | tf_op jit(solution)/shard_map/reduce_scatter | solution.py:193
  59.3 427.4 %reduce-scatter.11.cloned.1.call-start = ((), (), s32[]{:S(2)}) async-start(), calls=%async_computation.14 | async-start | bytes 23592960 | tf_op jit(solution)/shard_map/reduce_scatter | solution.py:257
  70.3 235.8 %copy-start.31 = (f32[1152]{0:T(1024)S(1)}, f32[1152]{0:T(1024)}, u32[]{:S(2)}) copy-start(f32[1152]{0:T(1024)} %param.28) | copy-start | bytes 13828
  70.3 445.6 %all-gather.16.cloned.1.call-start = ((), (), s32[]{:S(2)}) async-start(), calls=%async_computation.9 | async-start | bytes 2359296 | tf_op jit(solution)/shard_map/all_gather | solution.py:225
  71.2 239.9 %copy-start.20 = (f32[1024,16]{0,1:T(8,128)}, f32[1024,16]{0,1:T(8,128)S(1)}, u32[]{:S(2)}) copy-start(f32[1024,16]{0,1:T(8,128)S(1)} %get-tuple-element.404) | copy-start | bytes 196612
  71.2 239.9 %copy-start.22 = (f32[1024,16]{0,1:T(8,128)}, f32[1024,16]{0,1:T(8,128)S(1)}, u32[]{:S(2)}) copy-start(f32[1024,16]{0,1:T(8,128)S(1)} %get-tuple-element.405) | copy-start | bytes 196612
  312.9 231.8 %all-gather.18.cloned.1.call-start = ((), (), s32[]{:S(2)}) async-start(), calls=%async_computation.10 | async-start | bytes 2359296 | tf_op jit(solution)/shard_map/all_gather | solution.py:226
  315.7 787.9 %reduce-scatter.13.cloned.1.call-start = ((), (), s32[]{:S(2)}) async-start(), calls=%async_computation.15 | async-start | bytes 4718592 | tf_op jit(solution)/shard_map/reduce_scatter | solution.py:280
  1060.1 89.2 %reduce-scatter.15.cloned.1.call-start = ((), (), s32[]{:S(2)}) async-start(), calls=%async_computation.16 | async-start | bytes 4718592 | tf_op jit(solution)/shard_map/reduce_scatter | solution.py:281
  1060.9 170.3 %all-gather.26.cloned.1.call-start = ((), (), s32[]{:S(2)}) async-start(), calls=%async_computation.19 | async-start | bytes 9437184 | tf_op jit(solution)/shard_map/all_gather | solution.py:234
  1083.5 177.0 %all-gather.20.cloned.1.call-start = ((), (), s32[]{:S(2)}) async-start(), calls=%async_computation.11 | async-start | bytes 2359296 | tf_op jit(solution)/shard_map/all_gather | solution.py:233
  1087.1 255.2 %all-gather.28.cloned.1.call-start = ((), (), s32[]{:S(2)}) async-start(), calls=%async_computation.20 | async-start | bytes 9437184 | tf_op jit(solution)/shard_map/all_gather | solution.py:293
  1087.7 319.4 %all-gather.24.cloned.1.call-start = ((), (), s32[]{:S(2)}) async-start(), calls=%async_computation.17 | async-start | bytes 7077888 | tf_op jit(solution)/shard_map/all_gather | solution.py:292
  1153.8 106.7 %copy-start.16 = (bf16[384,384]{1,0:T(8,128)(2,1)S(1)}, bf16[384,384]{1,0:T(8,128)(2,1)}, u32[]{:S(2)}) copy-start(bf16[384,384]{1,0:T(8,128)(2,1)} %param.29) | copy-start | bytes 884740
  1153.8 328.8 %reduce-scatter.9.cloned.1.call-start = ((), (), s32[]{:S(2)}) async-start(), calls=%async_computation.12 | async-start | bytes 4718592 | tf_op jit(solution)/shard_map/reduce_scatter | solution.py:240
  1265.8 141.4 %copy-start.18 = (bf16[384,1152]{1,0:T(8,128)(2,1)S(1)}, bf16[384,1152]{1,0:T(8,128)(2,1)}, u32[]{:S(2)}) copy-start(bf16[384,1152]{1,0:T(8,128)(2,1)} %param.27) | copy-start | bytes 2654212
  1265.8 216.8 %reduce-scatter.17.cloned.1.call-start = ((), (), s32[]{:S(2)}) async-start(), calls=%async_computation.18 | async-start | bytes 9437184 | tf_op jit(solution)/shard_map/reduce_scatter | solution.py:305
  1415.0 266.5 %all-reduce.7.cloned.1.call-start = ((), (), s32[]{:S(2)}) async-start(), calls=%async_computation.21 | async-start | bytes 14155776 | tf_op jit(solution)/shard_map/psum | solution.py:337
  1440.1 42.6 %copy-start.7 = (bf16[1024,384]{1,0:T(8,128)(2,1)S(1)}, bf16[1024,384]{1,0:T(8,128)(2,1)}, u32[]{:S(2)}) copy-start(bf16[1024,384]{1,0:T(8,128)(2,1)} %param.24) | copy-start | bytes 2359300
  1440.1 42.5 %copy-start.26 = (f32[1024]{0:T(1024)S(1)}, f32[1024]{0:T(1024)}, u32[]{:S(2)}) copy-start(f32[1024]{0:T(1024)} %copy-done.25) | copy-start | bytes 12292
  1526.0 155.6 %copy-start.34 = (f32[384]{0:T(512)S(1)}, f32[384]{0:T(512)}, u32[]{:S(2)}) copy-start(f32[384]{0:T(512)} %get-tuple-element.716) | copy-start | bytes 4612
  (65 other events, 334.2 us)
Sparse Core Ops, SparseCore 0:
  18.3 11.5 all-gather.13
  32.0 10.9 all-gather.11
  44.6 10.9 all-gather.21
  59.4 246.6 reduce-scatter.6
  308.3 178.3 reduce-scatter.10
  488.7 27.1 all-gather.15
  517.4 27.1 all-gather.17
  1060.2 43.3 reduce-scatter.12
  1106.0 43.3 reduce-scatter.14
  1150.7 80.3 all-gather.25
  1233.3 27.2 all-gather.19
  1261.9 80.3 all-gather.27
  1344.4 62.6 all-gather.23
  1409.2 10.8 reduce-scatter.8
  1422.4 15.6 reduce-scatter.16
  1443.5 237.9 all-reduce.6
where the time goes:
time: 1710 us; the launch traced here: 1700 us
  waiting for transfers between devices  907 us (53%)
  matrix products  345 us (20%)
  local copies, waits for them, and re-layouts  189 us (11%)
  other arithmetic  91.2 us (5%)
  blocking collectives  84 us (5%)
  loops' own time  63.2 us (4%)
    reduce_scatter x1, waiting for transfers between devices, body(): lax.psum_scatter(jnp.concatenate([jnp.dot(first_all, w_qkv, preferred_ele...  235 us
    reduce_scatter x1, waiting for transfers between devices, body(): lax.psum_scatter(jnp.einsum('to,bjo->tbj', grad_all, stacked, preferred_e...  170 us
    psum x1, waiting for transfers between devices, body(): lax.psum((d_qkv, d_qkv_bias, d_dense, d_out_bias, d_in, d_in_bias, d_out)...  151 us
    all_gather x1, waiting for transfers between devices, body(): lax.all_gather(active[None], 'col', axis=0, tiled=True)  77.3 us
    all_gather x1, waiting for transfers between devices, body(): lax.all_gather(hidden_grad[None], 'col', axis=0, tiled=True)  76.5 us
    dot_general x24, matrix products, block_scores(): lax.dot_general(query_block, keys_here, (((1,), (1,)), ((), ())), preferr...  75.1 us
    all_gather x1, waiting for transfers between devices, body(): lax.all_gather(joined_grad[None], 'col', axis=0, tiled=True)  56.9 us
    dot_general x12, matrix products, one_block(): lax.dot_general(soft.astype(jnp.bfloat16), grad_block, (((0,), (0,)), (()...  52.3 us
  transfers between devices with their start and end apart: 16, of which 13 were waited for; matrix products, arithmetic and copies ran while one was open for 9% of the time, Pallas kernels for 0%

commit v1 on v0

v1 whole, which is shorter than its diff:
```python
import functools

import jax
import jax.numpy as jnp
from jax import lax
from jax.experimental import pallas as pl
from jax.experimental.pallas import tpu as pltpu
from jax.sharding import PartitionSpec as P

HEAD_DIM = 64
ROT = 16


norm_epsilon = 1e-05
masked_fill = -1e30


def rotary_tables(position):
    steps = jnp.arange(ROT // 2, dtype=jnp.int32).astype(jnp.float32)
    inverse = 10000.0 ** (-2.0 * steps / ROT)
    angle = position.astype(jnp.float32)[:, None] * inverse[None, :]
    angle = jnp.concatenate([angle, angle], axis=1)
    return (jnp.cos(angle), jnp.sin(angle))


def rotary(part, cosines, sines):
    turned = part[..., :ROT]
    swapped = jnp.concatenate([-turned[..., ROT // 2 :], turned[..., : ROT // 2]], axis=-1)
    rotated = turned * cosines[:, None, :] + swapped * sines[:, None, :]
    return jnp.concatenate([rotated, part[..., ROT:]], axis=-1)


def rotary_back(grads, cosines, sines):
    turned = grads[..., :ROT]
    scaled = turned * sines[:, None, :]
    swapped = jnp.concatenate([scaled[..., ROT // 2 :], -scaled[..., : ROT // 2]], axis=-1)
    return jnp.concatenate([turned * cosines[:, None, :] + swapped, grads[..., ROT:]], axis=-1)


def gelu_exact(values):
    return jax.nn.gelu(values, approximate=False)


BLOCK = 256
SWAP = [(0, 1), (1, 0)]


def attention_kernel(
    block, low_ref, seg_col, seg_row, q_ref, k_ref, v_ref, do_ref, ctx_ref, dq_ref, dk_ref, dv_ref
):
    heads, length, depth = q_ref.shape
    nt = (((1,), (1,)), ((), ()))
    tn = (((0,), (0,)), ((), ()))
    dk_ref[...] = jnp.zeros_like(dk_ref)
    dv_ref[...] = jnp.zeros_like(dv_ref)

    def query_step(i, carry):
        rows = pl.ds(pl.multiple_of(i * block, block), block)
        low = low_ref[i]
        segs = seg_col[rows, :]
        places = i * block + lax.broadcasted_iota(jnp.int32, (block, block), 0)
        queries = [q_ref[h, rows, :] for h in range(heads)]
        grads = [do_ref[h, rows, :] for h in range(heads)]

        def masked_scores(j, cols):
            key_places = j * block + lax.broadcasted_iota(jnp.int32, (block, block), 1)
            allowed = (segs == seg_row[j]) & (places >= key_places)
            return [
                jnp.where(
                    allowed,
                    lax.dot_general(
                        queries[h], k_ref[h, cols, :], nt, preferred_element_type=jnp.float32
                    ),
                    masked_fill,
                )
                for h in range(heads)
            ]

        def forward(j, state):
            cols = pl.ds(pl.multiple_of(j * block, block), block)
            scores = masked_scores(j, cols)
            out = []
            for h in range(heads):
                highest, total, acc = state[h]
                new = jnp.maximum(highest, jnp.max(scores[h], axis=1, keepdims=True))
                lifted = jnp.exp(scores[h] - new)
                shrink = jnp.exp(highest - new)
                total = total * shrink + jnp.sum(lifted, axis=1, keepdims=True)
                acc = acc * shrink + jnp.dot(
                    lifted.astype(jnp.bfloat16), v_ref[h, cols, :],
                    preferred_element_type=jnp.float32,
                )
                out.append((new, total, acc))
            return tuple(out)

        state = lax.fori_loop(
            low,
            i + 1,
            forward,
            tuple(
                (
                    jnp.full((block, 1), masked_fill, jnp.float32),
                    jnp.zeros((block, 1), jnp.float32),
                    jnp.zeros((block, depth), jnp.float32),
                )
                for _ in range(heads)
            ),
        )
        lse, inner = [], []
        for h in range(heads):
            highest, total, acc = state[h]
            context = acc / total
            ctx_ref[h, rows, :] = context.astype(jnp.bfloat16)
            lse.append(highest + jnp.log(total))
            inner.append(
                jnp.sum(context * grads[h].astype(jnp.float32), axis=1, keepdims=True)
            )

        def backward(j, state):
            cols = pl.ds(pl.multiple_of(j * block, block), block)
            scores = masked_scores(j, cols)
            out = []
            for h in range(heads):
                soft = jnp.exp(scores[h] - lse[h])
                grad_soft = lax.dot_general(
                    grads[h], v_ref[h, cols, :], nt, preferred_element_type=jnp.float32
                )
                grad_raw = (soft * (grad_soft - inner[h])).astype(jnp.bfloat16)
                out.append(
                    state[h]
                    + jnp.dot(grad_raw, k_ref[h, cols, :], preferred_element_type=jnp.float32)
                )
                dk_ref[h, cols, :] += lax.dot_general(
                    grad_raw, queries[h], tn, preferred_element_type=jnp.float32
                )
                dv_ref[h, cols, :] += lax.dot_general(
                    soft.astype(jnp.bfloat16), grads[h], tn, preferred_element_type=jnp.float32
                )
            return tuple(out)

        state = lax.fori_loop(
            low,
            i + 1,
            backward,
            tuple(jnp.zeros((block, depth), jnp.float32) for _ in range(heads)),
        )
        for h in range(heads):
            dq_ref[h, rows, :] = state[h] * HEAD_DIM ** (-0.5)
        return carry

    lax.fori_loop(0, length // block, query_step, 0)


def attention(queries, keys, values, grads, segments):
    heads, length, depth = queries.shape
    block = min(BLOCK, length)
    count = length // block
    firsts = segments.reshape(count, block)[:, 0]
    low = jnp.sum((segments[None, :] < firsts[:, None]).astype(jnp.int32), axis=1) // block
    vmem = pl.BlockSpec(memory_space=pltpu.VMEM)
    wide = jax.ShapeDtypeStruct((heads, length, depth), jnp.float32)
    return pl.pallas_call(
        functools.partial(attention_kernel, block),
        out_shape=(jax.ShapeDtypeStruct((heads, length, depth), jnp.bfloat16), wide, wide, wide),
        in_specs=[pl.BlockSpec(memory_space=pltpu.SMEM)] + [vmem] * 6,
        out_specs=(vmem,) * 4,
        compiler_params=pltpu.CompilerParams(vmem_limit_bytes=48 * 1024 * 1024),
        cost_estimate=pl.CostEstimate(
            flops=7 * 2 * heads * length * length // 4 * depth,
            bytes_accessed=heads * length * depth * 22,
            transcendentals=heads * length * length // 2,
        ),
    )(
        low,
        segments[:, None],
        segments.reshape(count, 1, block),
        queries,
        keys,
        values,
        grads,
    )


def in_order(index, mine, other, axis=0):
    return jnp.where(
        index == 0,
        jnp.concatenate([mine, other], axis=axis),
        jnp.concatenate([other, mine], axis=axis),
    )


def body(
    tokens,
    segments,
    positions,
    w_qkv,
    b_qkv,
    w_dense,
    b_dense,
    w_in,
    b_in,
    w_out,
    b_out,
    gain_one,
    shift_one,
    gain_two,
    shift_two,
    cotangent,
):
    rows_here, width = tokens.shape
    features = 2 * width
    length = segments.shape[0]
    row, col = lax.axis_index("row"), lax.axis_index("col")
    f32, bf16 = jnp.float32, jnp.bfloat16

    def swap_col(part):
        return lax.ppermute(part, "col", SWAP)

    def swap_row(part):
        return lax.ppermute(part, "row", SWAP)

    def split_half(array, axis):
        half = array.shape[axis] // 2
        mine = lax.dynamic_slice_in_dim(array, col * half, half, axis)
        other = lax.dynamic_slice_in_dim(array, (1 - col) * half, half, axis)
        return mine, other

    def whole_rows(part):
        wide = jnp.concatenate([part, swap_col(part)], axis=1)
        return in_order(row, wide, swap_row(wide))

    x_all = whole_rows(tokens)
    norms = jnp.stack([gain_one, shift_one, gain_two, shift_two])
    norms = jnp.concatenate([norms, swap_col(norms)], axis=1)

    qkv_mine, qkv_other = split_half(w_qkv, 1)
    qkv_w = jnp.concatenate([qkv_mine, swap_col(qkv_other)], axis=0)
    g_all = whole_rows(cotangent)
    dense_mine, dense_other = split_half(w_dense, 0)
    dense_w = jnp.concatenate([dense_mine, swap_col(dense_other)], axis=1)
    in_mine, in_other = split_half(w_in, 1)
    in_w = jnp.concatenate([in_mine, swap_col(in_other)], axis=0)
    out_mine, out_other = split_half(w_out, 0)
    out_w = jnp.concatenate([out_mine, swap_col(out_other)], axis=1)

    inputs = x_all.astype(f32)
    average = jnp.mean(inputs, axis=1, keepdims=True)
    spread = jnp.mean(inputs * inputs, axis=1, keepdims=True) - average * average
    inv_std = lax.rsqrt(spread + norm_epsilon)
    normed = (inputs - average) * inv_std
    first_in = (normed * norms[0] + norms[1]).astype(bf16)
    second_in = (normed * norms[2] + norms[3]).astype(bf16)

    joined = jnp.dot(first_in, qkv_w, preferred_element_type=f32) + split_half(b_qkv, 0)[0]
    joined = joined.reshape(length, -1, 3, HEAD_DIM)
    cosines, sines = rotary_tables(positions)
    query_heads = jnp.transpose(
        (rotary(joined[:, :, 0], cosines, sines)).astype(bf16) * bf16(HEAD_DIM ** (-0.5)),
        (1, 0, 2),
    )
    key_heads = jnp.transpose(rotary(joined[:, :, 1], cosines, sines).astype(bf16), (1, 0, 2))
    value_heads = jnp.transpose(joined[:, :, 2].astype(bf16), (1, 0, 2))
    d_context = jnp.dot(g_all, dense_w.T, preferred_element_type=f32).astype(bf16)
    grad_heads = jnp.transpose(d_context.reshape(length, -1, HEAD_DIM), (1, 0, 2))
    contexts, query_grads, key_grads, value_grads = attention(
        query_heads, key_heads, value_heads, grad_heads, segments
    )
    context = jnp.transpose(contexts, (1, 0, 2)).reshape(length, -1)

    hidden = jnp.dot(second_in, in_w, preferred_element_type=f32) + split_half(b_in, 0)[0]
    active = gelu_exact(hidden).astype(bf16)
    d_active = jnp.dot(g_all, out_w.T, preferred_element_type=f32)
    d_hidden = jax.vjp(gelu_exact, hidden)[1](d_active)[0].astype(bf16)

    def tn_dot(left, right):
        return lax.dot_general(left, right, (((0,), (0,)), ((), ())), preferred_element_type=f32)

    def own_rows(partial):
        mine = lax.dynamic_slice_in_dim(partial, row * rows_here, rows_here, 0)
        other = lax.dynamic_slice_in_dim(partial, (1 - row) * rows_here, rows_here, 0)
        return mine + swap_row(other.astype(bf16)).astype(f32)

    def own_block(summed):
        return summed[:, :width] + swap_col(summed[:, width:].astype(bf16)).astype(f32)

    def pack_sum(mine, other, axis):
        both = in_order(col, mine.astype(bf16), swap_col(other.astype(bf16)), axis)
        return lax.psum(both, "dp").astype(f32)

    d_out = tn_dot(active, g_all)
    d_out = pack_sum(d_out[:, :width], d_out[:, width:], 0)
    d_in = tn_dot(second_in, d_hidden)
    d_in = pack_sum(d_in[:width], d_in[width:], 1)
    d_dense = tn_dot(context, g_all)
    d_dense = pack_sum(d_dense[:, :width], d_dense[:, width:], 0)

    query_back = rotary_back(jnp.transpose(query_grads, (1, 0, 2)), cosines, sines)
    key_back = rotary_back(jnp.transpose(key_grads, (1, 0, 2)), cosines, sines)
    value_back = jnp.transpose(value_grads, (1, 0, 2))
    d_joined = (
        jnp.stack([query_back, key_back, value_back], axis=2).reshape(length, -1).astype(bf16)
    )
    d_qkv = tn_dot(first_in, d_joined)
    d_qkv = pack_sum(d_qkv[:width], d_qkv[width:], 1)

    branches = own_block(
        own_rows(
            jnp.dot(context, dense_w, preferred_element_type=f32)
            + jnp.dot(active, out_w, preferred_element_type=f32)
        )
    )
    mixed = tokens.astype(f32) + branches + b_dense + b_out

    d_first = lax.dot_general(d_joined, qkv_w, (((1,), (1,)), ((), ())), preferred_element_type=f32)
    d_second = lax.dot_general(d_hidden, in_w, (((1,), (1,)), ((), ())), preferred_element_type=f32)
    hat = own_rows(d_first * norms[0] + d_second * norms[2])
    own_inputs = lax.dynamic_slice_in_dim(x_all, row * rows_here, rows_here, 0).astype(f32)
    own_average = lax.dynamic_slice_in_dim(average, row * rows_here, rows_here, 0)
    own_std = lax.dynamic_slice_in_dim(inv_std, row * rows_here, rows_here, 0)
    own_normed = (own_inputs - own_average) * own_std
    hat_sums = jnp.stack([jnp.sum(hat, axis=1), jnp.sum(hat * own_normed, axis=1)])
    hat_means = (hat_sums + swap_col(hat_sums)) / features
    d_tokens = cotangent.astype(f32) + own_std * (
        own_block(hat)
        - hat_means[0][:, None]
        - own_normed[:, :width] * hat_means[1][:, None]
    )

    vectors = jnp.stack(
        [
            jnp.sum(d_first * normed, axis=0),
            jnp.sum(d_first, axis=0),
            jnp.sum(d_second * normed, axis=0),
            jnp.sum(d_second, axis=0),
        ]
    )
    vectors = vectors[:, :width] + swap_col(vectors[:, width:])
    vectors = jnp.concatenate([vectors, jnp.sum(cotangent, axis=0, dtype=f32)[None]], axis=0)
    vectors = vectors + swap_row(vectors)
    biases = jnp.concatenate(
        [jnp.sum(d_joined, axis=0, dtype=f32), jnp.sum(d_hidden, axis=0, dtype=f32)]
    )
    other_biases = swap_col(biases)
    small = lax.psum(jnp.concatenate([vectors.reshape(-1), biases, other_biases]), "dp")
    vectors = small[: 5 * width].reshape(5, width)
    total = biases.shape[0]
    own_bias = small[5 * width : 5 * width + total]
    other_bias = small[5 * width + total :]
    cut = d_joined.shape[1]
    d_qkv_bias = in_order(col, own_bias[:cut], other_bias[:cut])
    d_in_bias = in_order(col, own_bias[cut:], other_bias[cut:])
    return (
        mixed,
        d_tokens,
        d_qkv,
        d_qkv_bias,
        d_dense,
        vectors[4],
        d_in,
        d_in_bias,
        d_out,
        vectors[4],
        vectors[0],
        vectors[1],
        vectors[2],
        vectors[3],
    )


def solution(mesh):
    in_specs = (
        P(("dp", "row"), "col"),
        P("dp"),
        P("dp"),
        P("col", "row"),
        P("row"),
        P("row", "col"),
        P("col"),
        P("col", "row"),
        P("row"),
        P("row", "col"),
        P("col"),
        P("col"),
        P("col"),
        P("col"),
        P("col"),
        P(("dp", "row"), "col"),
    )
    out_specs = (
        P(("dp", "row"), "col"),
        P(("dp", "row"), "col"),
        P("col", "row"),
        P("row"),
        P("row", "col"),
        P("col"),
        P("col", "row"),
        P("row"),
        P("row", "col"),
        P("col"),
        P("col"),
        P("col"),
        P("col"),
        P("col"),
    )
    return jax.shard_map(body, mesh=mesh, in_specs=in_specs, out_specs=out_specs, check_vma=False)
```

time: 1710 us -> 475 us (0.28)
  waiting for transfers between devices: 907 us -> 134 us
  matrix products: 345 us -> 71.4 us
  local copies, waits for them, and re-layouts: 189 us -> 77.2 us
  loops' own time: 63.2 us -> 0 us
  Pallas kernels: 0 us -> 59.5 us
  blocking collectives: 84 us -> 34.6 us
  other arithmetic: 91.2 us -> 58.6 us
  starting transfers between devices: 1.5 us -> 20.2 us
    reduce_scatter x6 -> x0, waiting for transfers between devices: 459 us -> none  [the longest x1 235 us: body(): lax.psum_scatter(jnp.concatenate([jnp.dot(first_all, w_qkv, preferred_ele...]
    all_gather x9 -> x0, waiting for transfers between devices: 294 us -> none  [the longest x1 77.3 us: body(): lax.all_gather(active[None], 'col', axis=0, tiled=True)]
    dot_general x95 -> x12, matrix products: 345 us -> 71.4 us  [the longest x1 20.3 us: body(): jnp.dot(second_in, in_w, preferred_element_type=f32)]
    psum x1, waiting for transfers between devices: 151 us -> 60.8 us  [pack_sum(): return lax.psum(both, 'dp').astype(f32)]
    ppermute x0 -> x21, waiting for transfers between devices: none -> 72.8 us  [the longest x16 72.7 us: swap_col(): return lax.ppermute(part, 'col', SWAP)]
    another operation x2 -> x0, loops' own time: 63.2 us -> none  [the longest x1 31.8 us: attend_backward(): lax.scan(one_block, (zeros_like_keys, zeros_like_keys), elements)]
    dynamic_update_slice x36 -> x0, local copies, waits for them, and re-layouts: 62.8 us -> none  [the longest x24 46.7 us: attend_backward(): lax.scan(one_block, (zeros_like_keys, zeros_like_keys), elements)]
    pallas_call x0 -> x1, Pallas kernels: none -> 59.5 us  [attention(): pl.pallas_call(functools.partial(attention_kernel, block), out_shape=(jax...]
  transfers between devices with their start and end apart: 16 -> 22, of which waited for: 13 -> 8; matrix products, arithmetic and copies ran while one was open for 9% -> 35% of each run, Pallas kernels for 0% -> 13%
where the time goes in v1:
time: 475 us; the launch traced here: 470 us
  waiting for transfers between devices  134 us (28%)
  local copies, waits for them, and re-layouts  77.2 us (16%)
  matrix products  71.4 us (15%)
  Pallas kernels  59.5 us (13%)
  other arithmetic  58.6 us (12%)
  blocking collectives  34.6 us (7%)
  starting transfers between devices  20.2 us (4%)
  between operations  15.1 us (3%)
    ppermute x16, waiting for transfers between devices, swap_col(): return lax.ppermute(part, 'col', SWAP)  72.7 us
    psum x1, waiting for transfers between devices, pack_sum(): return lax.psum(both, 'dp').astype(f32)  60.8 us
    pallas_call x1, Pallas kernels, attention(): pl.pallas_call(functools.partial(attention_kernel, block), out_shape=(jax...  59.5 us
    psum x1, blocking collectives, body(): lax.psum(jnp.concatenate([vectors.reshape(-1), biases, other_biases]), 'dp')  34.6 us
    unnamed x96, local copies, waits for them, and re-layouts  21.4 us
    dot_general x1, matrix products, body(): jnp.dot(second_in, in_w, preferred_element_type=f32)  20.3 us
    ppermute x16, starting transfers between devices, swap_col(): return lax.ppermute(part, 'col', SWAP)  19.6 us
    dot_general x4, matrix products, tn_dot(): lax.dot_general(left, right, (((0,), (0,)), ((), ())), preferred_element_...  16 us
  transfers between devices with their start and end apart: 22, of which 8 were waited for; matrix products, arithmetic and copies ran while one was open for 35% of the time, Pallas kernels for 13%

profile of v1, /device:TPU:0, one launch (start us, length us, event | category | flops | bytes accessed | tf_op | source)
XLA Modules:
  0.0 470.1 jit_solution(17694623293773631264)
XLA Ops:
  41.6 18.0 %collective-permute-done.4 = bf16[1024,384]{1,0:T(8,128)(2,1)} collective-permute-done((bf16[1024,384]{1,0:T(8,128)(2,1)}, bf16[1024,384]{1,0:T(8,128)(2,1)}, u32[]{:S(2)}, u32[]{:S(2)}) %collective-permute-start.4) | collective-permute-done | bytes 786464 | tf_op jit(solution)/shard_map/ppermute | solution.py:217
  63.8 4.1 convert_reduce_fusion
  68.0 4.1 convolution_add_fusion.1
  78.6 6.5 %slice_negate_fusion.3 = (f32[2048,3,8]{2,0,1:T(8,128)}, f32[2048,3,8]{2,0,1:T(8,128)}) fusion(f32[2048,3,64]{2,0,1:T(8,128)} %bitcast.41), kind=kLoop, calls=%fused_computation.45 | loop fusion | flops 49152 | bytes 786432 | tf_op jit(solution)/shard_map/neg | solution.py:28
  93.0 6.5 %slice_negate_fusion.2 = (f32[2048,3,8]{2,0,1:T(8,128)}, f32[2048,3,8]{2,0,1:T(8,128)}) fusion(f32[2048,3,64]{2,0,1:T(8,128)} %bitcast.44), kind=kLoop, calls=%fused_computation.40 | loop fusion | flops 49152 | bytes 786432 | tf_op jit(solution)/shard_map/neg | solution.py:28
  105.0 3.8 slice.335
  118.7 4.4 convolution_convert_fusion
  124.8 5.6 %fusion.19 = (bf16[2048,3,16]{2,0,1:T(8,128)(2,1)S(1)}, bf16[2048,3,16]{2,0,1:T(8,128)(2,1)S(1)}) fusion(f32[2048,3,16]{2,0,1:T(8,128)} %copy.132, f32[2048,3,64]{2,0,1:T(8,128)} %bitcast.46, f32[2048,16]{1,0:T(8,128)S(1)} %copy.122, f32[2048,3,16]{2,0,1:T(8,128)} %copy.127, f32[2048,3,64]{2,0,1:T(8,128)} %bitcast.42), kind=kLoop, calls=%fused_computation.43 | loop fusion | flops 589824 | bytes 2097152 | tf_op jit(solution)/shard_map/convert.11
  132.3 59.5 %shard_map.263 = (bf16[3,2048,64]{2,1,0:T(8,128)(2,1)S(1)}, f32[3,2048,64]{2,1,0:T(8,128)}, f32[3,2048,64]{2,1,0:T(8,128)}, f32[3,2048,64]{2,1,0:T(8,128)}) custom-call(s32[8]{0:T(128)S(1)} %and_select_fusion.low_ref, s32[2048,1]{1,0:T(8,128)S(1)} %copy.135.seg_col, s32[8,1,256]{2,1,0:T(1,128)S(1)} %bitcast.40, ...), custom_call_target="tpu_custom_call" | custom-call | flops 2818572288 | bytes 8650752 | tf_op jit(solution)/shard_map/pallas_call | solution.py:162
  204.0 20.3 %multiply_convert_fusion = (bf16[2048,768]{1,0:T(8,128)(2,1)}, f32[2048,768]{1,0:T(8,128)}, f32[2048,768]{1,0:T(8,128)}) fusion(f32[768]{0:T(1024)S(1)} %dynamic_slice.56, bf16[384,768]{1,0:T(8,128)(2,1)} %collective-permute-done.7, bf16[384,768]{1,0:T(8,128)(2,1)S(1)} %copy-done.27, bf16[2048,768]{1,0:T(8,128)(2,1)S(1)} %copy-done.8, ...), kind=kOutput, calls=%fused_computation.22 | convolution fusion | flops 2531524608 | bytes 20079616 | tf_op jit(solution)/shard_map/dot_general | solution.py:270
  229.2 6.1 %copy.137 = bf16[2048,3,3,64]{0,3,2,1:T(8,128)(2,1)} copy(bf16[2048,3,3,64]{3,0,1,2:T(8,128)(2,1)} %get-tuple-element.139) | data formatting | bytes 4718592 | tf_op jit(solution)/shard_map/convert_element_type | solution.py:301
  235.3 10.9 %convert_reduce_fusion.2 = (f32[768]{0:T(1024)S(1)}, bf16[2048,768]{1,0:T(8,128)(2,1)S(1)}) fusion(f32[2048,768]{1,0:T(8,128)} %get-tuple-element.142, bf16[768,384]{1,0:T(8,128)(2,1)} %collective-permute-done.8, bf16[768,384]{1,0:T(8,128)(2,1)S(1)} %copy-done.25, bf16[1024,768]{1,0:T(8,128)(2,1)} %collective-permute-done.5, ...), kind=kOutput, calls=%fused_computation.19 | convolution fusion | flops 2459172096 | bytes 20060160 | tf_op jit(solution)/shard_map/dot_general | solution.py:272
  246.2 4.7 convolution_convert_fusion.2
  253.3 3.8 fusion.31
  257.1 6.3 %fusion.9 = (f32[768]{0:T(1024)S(1)}, f32[768]{0:T(1024)S(1)}, f32[768]{0:T(1024)S(1)}, f32[768]{0:T(1024)S(1)}, f32[2048,768]{1,0:T(8,128)S(1)}) fusion(bf16[2048,768]{1,0:T(8,128)(2,1)S(1)} %copy-done.9, f32[2048]{0:T(1024)S(1)} %get-tuple-element.196, f32[2048]{0:T(1024)S(1)} %get-tuple-element.195, f32[2048,768]{1,0:T(8,128)S(1)} %fusion.31, ...), kind=kOutput, calls=%fused_computation.15 | convolution fusion | flops 1832580096 | bytes 19007488 | tf_op jit(solution)/shard_map/dot_general | solution.py:314
  268.5 4.1 convolution_convert_fusion.4
  275.2 4.8 %convolution_convert_fusion.1 = bf16[768,768]{1,0:T(8,128)(2,1)S(1)} fusion(bf16[2048,768]{1,0:T(8,128)(2,1)S(1)} %copy-done.41, bf16[1024,768]{1,0:T(8,128)(2,1)} %collective-permute-done.5, bf16[1024,768]{1,0:T(8,128)(2,1)S(1)} %copy-done.33, pred[]{:T(512)S(6)} %eq.4), kind=kOutput, calls=%fused_computation.82 | convolution fusion | flops 2430664704 | bytes 7471105 | tf_op jit(solution)/shard_map/dot_general | solution.py:276
  290.2 11.4 %collective-permute-done.14 = bf16[384,576]{0,1:T(8,128)(2,1)S(1)} collective-permute-done((bf16[384,576]{0,1:T(8,128)(2,1)S(1)}, bf16[384,576]{0,1:T(8,128)(2,1)S(1)}, u32[]{:S(2)}, u32[]{:S(2)}) %collective-permute-start.14) | collective-permute-done | bytes 442400 | tf_op jit(solution)/shard_map/ppermute | solution.py:217
  304.3 9.0 %collective-permute-done.20 = bf16[768,384]{1,0:T(8,128)(2,1)S(1)} collective-permute-done((bf16[768,384]{1,0:T(8,128)(2,1)S(1)}, bf16[768,384]{1,0:T(8,128)(2,1)S(1)}, u32[]{:S(2)}, u32[]{:S(2)}) %collective-permute-start.20) | collective-permute-done | bytes 589856 | tf_op jit(solution)/shard_map/ppermute | solution.py:217
  316.1 4.2 fusion.49
  326.0 15.1 %collective-permute-done.13 = f32[2,1024]{1,0:T(2,128)S(1)} collective-permute-done((f32[2,1024]{1,0:T(2,128)S(1)}, f32[2,1024]{1,0:T(2,128)S(1)}, u32[]{:S(2)}, u32[]{:S(2)}) %collective-permute-start.13) | collective-permute-done | bytes 8224 | tf_op jit(solution)/shard_map/ppermute | solution.py:217
  343.1 13.0 %collective-permute-done.10 = bf16[1024,384]{1,0:T(8,128)(2,1)S(1)} collective-permute-done((bf16[1024,384]{1,0:T(8,128)(2,1)S(1)}, bf16[1024,384]{1,0:T(8,128)(2,1)S(1)}, u32[]{:S(2)}, u32[]{:S(2)}) %collective-permute-start.10) | collective-permute-done | bytes 786464 | tf_op jit(solution)/shard_map/ppermute | solution.py:217
  357.7 34.6 %psum.36 = f32[4608]{0:T(1024)S(1)} all-reduce(f32[4608]{0:T(1024)S(1)} %concatenate.140), channel_id=1, replica_groups=mesh['dp'=8,'row'=2,'col'=2] {'dp'}, use_global_device_ids=true, to_apply=%region_13.14 | all-reduce | flops 4608 | bytes 36864 | tf_op jit(solution)/shard_map/psum | solution.py:344
  394.4 60.8 %all-reduce.3.cloned.1.call-done = (bf16[384,1152]{0,1:T(8,128)(2,1)}, bf16[384,1536]{0,1:T(8,128)(2,1)}, bf16[384,384]{1,0:T(8,128)(2,1)}, bf16[1536,384]{1,0:T(8,128)(2,1)}) async-done(((bf16[384,1152]{0,1:T(8,128)(2,1)}, bf16[384,1536]{0,1:T(8,128)(2,1)}, bf16[384,384]{1,0:T(8,128)(2,1)}, bf16[1536,384]{1,0:T(8,128)(2,1)}), (bf16[384,1152]{0,1:T(8,128)(2,1)}, bf16[384,1536]{0,1:T(8,128)(2,1)}, ...) | async-done | bytes 3538960 | tf_op jit(solution)/shard_map/psum | solution.py:288
  (230 shorter events, 133.6 us)
Async XLA Ops:
  7.2 448.0 %all-reduce.3.cloned.1.call-start = ((), (), s32[]{:S(2)}) async-start(), calls=%async_computation | async-start | bytes 7077888 | tf_op jit(solution)/shard_map/psum | solution.py:288
  7.2 21.7 %collective-permute-start = (bf16[1024,384]{1,0:T(8,128)(2,1)}, bf16[1024,384]{1,0:T(8,128)(2,1)}, u32[]{:S(2)}, u32[]{:S(2)}) collective-permute-start(bf16[1024,384]{1,0:T(8,128)(2,1)} %param.16), channel_id=1, source_target_pairs={{0,1},{1,0},{2,3},{3,2},{4,5},{5,4},{6,7},{7,6},{8,9},{9,8},{10,11... | collective-permute-start | bytes 2359304 | tf_op jit(solution)/shard_map/ppermute | solution.py:217
  12.9 55.1 %collective-permute-start.3 = (bf16[384,576]{1,0:T(8,128)(2,1)}, bf16[384,576]{1,0:T(8,128)(2,1)}, u32[]{:S(2)}, u32[]{:S(2)}) collective-permute-start(bf16[384,576]{1,0:T(8,128)(2,1)} %get-tuple-element.173), channel_id=1, source_target_pairs={{0,1},{1,0},{2,3},{3,2},{4,5},{5,4},{6,7},{7,6},{8,9},{9,8},{10,11... | collective-permute-start | bytes 1327112 | tf_op jit(solution)/shard_map/ppermute | solution.py:217
  15.8 23.8 %collective-permute-start.2 = (f32[4,384]{1,0:T(4,128)S(1)}, f32[4,384]{1,0:T(4,128)S(1)}, u32[]{:S(2)}, u32[]{:S(2)}) collective-permute-start(f32[4,384]{1,0:T(4,128)S(1)} %pad_maximum_fusion.20), channel_id=1, source_target_pairs={{0,1},{1,0},{2,3},{3,2},{4,5},{5,4},{6,7},{7,6},{8,9},{9,8},{10,11... | collective-permute-start | bytes 18440 | tf_op jit(solution)/shard_map/ppermute | solution.py:217
  19.4 99.3 %collective-permute-start.6 = (bf16[192,384]{1,0:T(8,128)(2,1)}, bf16[192,384]{1,0:T(8,128)(2,1)}, u32[]{:S(2)}, u32[]{:S(2)}) collective-permute-start(bf16[192,384]{1,0:T(8,128)(2,1)} %get-tuple-element.179), channel_id=1, source_target_pairs={{0,1},{1,0},{2,3},{3,2},{4,5},{5,4},{6,7},{7,6},{8,9},{9,8},{10,11... | collective-permute-start | bytes 442376 | tf_op jit(solution)/shard_map/ppermute | solution.py:217
  19.6 40.1 %collective-permute-start.4 = (bf16[1024,384]{1,0:T(8,128)(2,1)}, bf16[1024,384]{1,0:T(8,128)(2,1)}, u32[]{:S(2)}, u32[]{:S(2)}) collective-permute-start(bf16[1024,384]{1,0:T(8,128)(2,1)} %param.31), channel_id=1, source_target_pairs={{0,1},{1,0},{2,3},{3,2},{4,5},{5,4},{6,7},{7,6},{8,9},{9,8},{10,11... | collective-permute-start | bytes 2359304 | tf_op jit(solution)/shard_map/ppermute | solution.py:217
  31.1 32.7 %collective-permute-start.1 = (bf16[1024,768]{1,0:T(8,128)(2,1)}, bf16[1024,768]{1,0:T(8,128)(2,1)}, u32[]{:S(2)}, u32[]{:S(2)}) collective-permute-start(bf16[1024,768]{1,0:T(8,128)(2,1)} %constant_dynamic-update-slice_fusion), channel_id=1, source_target_pairs={{0,2},{2,0},{1,3},{3,1},{4,6},{6,4},{5,7},{7,5},{8,10},{10,8},{9,1... | collective-permute-start | bytes 4718600 | tf_op jit(solution)/shard_map/ppermute | solution.py:220
  35.2 89.6 %copy-start.5 = (f32[2048,16]{1,0:T(8,128)}, f32[2048,16]{1,0:T(8,128)S(1)}, u32[]{:S(2)}) copy-start(f32[2048,16]{1,0:T(8,128)S(1)} %copy.122) | copy-start | bytes 393220
  39.5 163.4 %collective-permute-start.7 = (bf16[384,768]{1,0:T(8,128)(2,1)}, bf16[384,768]{1,0:T(8,128)(2,1)}, u32[]{:S(2)}, u32[]{:S(2)}) collective-permute-start(bf16[384,768]{1,0:T(8,128)(2,1)} %get-tuple-element.163), channel_id=1, source_target_pairs={{0,1},{1,0},{2,3},{3,2},{4,5},{5,4},{6,7},{7,6},{8,9},{9,8},{10,11... | collective-permute-start | bytes 1769480 | tf_op jit(solution)/shard_map/ppermute | solution.py:217
  59.6 175.6 %collective-permute-start.8 = (bf16[768,384]{1,0:T(8,128)(2,1)}, bf16[768,384]{1,0:T(8,128)(2,1)}, u32[]{:S(2)}, u32[]{:S(2)}) collective-permute-start(bf16[768,384]{1,0:T(8,128)(2,1)} %get-tuple-element.161), channel_id=1, source_target_pairs={{0,1},{1,0},{2,3},{3,2},{4,5},{5,4},{6,7},{7,6},{8,9},{9,8},{10,11... | collective-permute-start | bytes 1769480 | tf_op jit(solution)/shard_map/ppermute | solution.py:217
  63.8 54.9 %collective-permute-start.5 = (bf16[1024,768]{1,0:T(8,128)(2,1)}, bf16[1024,768]{1,0:T(8,128)(2,1)}, u32[]{:S(2)}, u32[]{:S(2)}) collective-permute-start(bf16[1024,768]{1,0:T(8,128)(2,1)} %constant_dynamic-update-slice_fusion.2), channel_id=1, source_target_pairs={{0,2},{2,0},{1,3},{3,1},{4,6},{6,4},{5,7},{7,5},{8,10},{10,8},{9,1... | collective-permute-start | bytes 4718600 | tf_op jit(solution)/shard_map/ppermute | solution.py:220
  264.2 51.0 %collective-permute-start.15 = (f32[4,384]{1,0:T(4,128)}, f32[4,384]{1,0:T(4,128)}, u32[]{:S(2)}, u32[]{:S(2)}) collective-permute-start(f32[4,384]{1,0:T(4,128)} %slice.271), channel_id=1, source_target_pairs={{0,1},{1,0},{2,3},{3,2},{4,5},{5,4},{6,7},{7,6},{8,9},{9,8},{10,11... | collective-permute-start | bytes 18440 | tf_op jit(solution)/shard_map/ppermute | solution.py:217
  267.3 48.7 %collective-permute-start.11 = (bf16[1024,768]{1,0:T(8,128)(2,1)}, bf16[1024,768]{1,0:T(8,128)(2,1)}, u32[]{:S(2)}, u32[]{:S(2)}) collective-permute-start(bf16[1024,768]{1,0:T(8,128)(2,1)} %dynamic-slice_convert_fusion), channel_id=1, source_target_pairs={{0,2},{2,0},{1,3},{3,1},{4,6},{6,4},{5,7},{7,5},{8,10},{10,8},{9,1... | collective-permute-start | bytes 4718600 | tf_op jit(solution)/shard_map/ppermute | solution.py:220
  272.7 14.7 %collective-permute-start.18 = (bf16[192,384]{1,0:T(8,128)(2,1)S(1)}, bf16[192,384]{1,0:T(8,128)(2,1)S(1)}, u32[]{:S(2)}, u32[]{:S(2)}) collective-permute-start(bf16[192,384]{1,0:T(8,128)(2,1)S(1)} %get-tuple-element.177), channel_id=1, source_target_pairs={{0,1},{1,0},{2,3},{3,2},{4,5},{5,4},{6,7},{7,6},{8,9},{9,8},{10,11... | collective-permute-start | bytes 442376 | tf_op jit(solution)/shard_map/ppermute | solution.py:217
  272.9 30.0 %collective-permute-start.19 = (bf16[384,768]{0,1:T(8,128)(2,1)S(1)}, bf16[384,768]{0,1:T(8,128)(2,1)S(1)}, u32[]{:S(2)}, u32[]{:S(2)}) collective-permute-start(bf16[384,768]{0,1:T(8,128)(2,1)S(1)} %get-tuple-element.159), channel_id=1, source_target_pairs={{0,1},{1,0},{2,3},{3,2},{4,5},{5,4},{6,7},{7,6},{8,9},{9,8},{10,11... | collective-permute-start | bytes 1769480 | tf_op jit(solution)/shard_map/ppermute | solution.py:217
  275.1 26.5 %collective-permute-start.14 = (bf16[384,576]{0,1:T(8,128)(2,1)S(1)}, bf16[384,576]{0,1:T(8,128)(2,1)S(1)}, u32[]{:S(2)}, u32[]{:S(2)}) collective-permute-start(bf16[384,576]{0,1:T(8,128)(2,1)S(1)} %get-tuple-element.171), channel_id=1, source_target_pairs={{0,1},{1,0},{2,3},{3,2},{4,5},{5,4},{6,7},{7,6},{8,9},{9,8},{10,11... | collective-permute-start | bytes 1327112 | tf_op jit(solution)/shard_map/ppermute | solution.py:217
  287.4 25.9 %collective-permute-start.20 = (bf16[768,384]{1,0:T(8,128)(2,1)S(1)}, bf16[768,384]{1,0:T(8,128)(2,1)S(1)}, u32[]{:S(2)}, u32[]{:S(2)}) collective-permute-start(bf16[768,384]{1,0:T(8,128)(2,1)S(1)} %get-tuple-element.157), channel_id=1, source_target_pairs={{0,1},{1,0},{2,3},{3,2},{4,5},{5,4},{6,7},{7,6},{8,9},{9,8},{10,11... | collective-permute-start | bytes 1769480 | tf_op jit(solution)/shard_map/ppermute | solution.py:217
  301.6 20.9 %collective-permute-start.9 = (bf16[1024,768]{1,0:T(8,128)(2,1)}, bf16[1024,768]{1,0:T(8,128)(2,1)}, u32[]{:S(2)}, u32[]{:S(2)}) collective-permute-start(bf16[1024,768]{1,0:T(8,128)(2,1)} %dynamic-slice_convert_fusion.1), channel_id=1, source_target_pairs={{0,2},{2,0},{1,3},{3,1},{4,6},{6,4},{5,7},{7,5},{8,10},{10,8},{9,1... | collective-permute-start | bytes 4718600 | tf_op jit(solution)/shard_map/ppermute | solution.py:220
  314.8 42.8 %collective-permute-start.17 = (f32[1344]{0:T(1024)S(1)}, f32[1344]{0:T(1024)S(1)}, u32[]{:S(2)}, u32[]{:S(2)}) collective-permute-start(f32[1344]{0:T(1024)S(1)} %pad_maximum_fusion.19), channel_id=1, source_target_pairs={{0,1},{1,0},{2,3},{3,2},{4,5},{5,4},{6,7},{7,6},{8,9},{9,8},{10,11... | collective-permute-start | bytes 16136 | tf_op jit(solution)/shard_map/ppermute | solution.py:217
  320.4 20.8 %collective-permute-start.12 = (bf16[1024,384]{1,0:T(8,128)(2,1)S(1)}, bf16[1024,384]{1,0:T(8,128)(2,1)S(1)}, u32[]{:S(2)}, u32[]{:S(2)}) collective-permute-start(bf16[1024,384]{1,0:T(8,128)(2,1)S(1)} %slice.337), channel_id=1, source_target_pairs={{0,1},{1,0},{2,3},{3,2},{4,5},{5,4},{6,7},{7,6},{8,9},{9,8},{10,11... | collective-permute-start | bytes 2359304 | tf_op jit(solution)/shard_map/ppermute | solution.py:217
  322.0 19.1 %collective-permute-start.13 = (f32[2,1024]{1,0:T(2,128)S(1)}, f32[2,1024]{1,0:T(2,128)S(1)}, u32[]{:S(2)}, u32[]{:S(2)}) collective-permute-start(f32[2,1024]{1,0:T(2,128)S(1)} %pad_maximum_fusion.18), channel_id=1, source_target_pairs={{0,1},{1,0},{2,3},{3,2},{4,5},{5,4},{6,7},{7,6},{8,9},{9,8},{10,11... | collective-permute-start | bytes 24584 | tf_op jit(solution)/shard_map/ppermute | solution.py:217
  324.4 31.7 %collective-permute-start.10 = (bf16[1024,384]{1,0:T(8,128)(2,1)S(1)}, bf16[1024,384]{1,0:T(8,128)(2,1)S(1)}, u32[]{:S(2)}, u32[]{:S(2)}) collective-permute-start(bf16[1024,384]{1,0:T(8,128)(2,1)S(1)} %slice.338), channel_id=1, source_target_pairs={{0,1},{1,0},{2,3},{3,2},{4,5},{5,4},{6,7},{7,6},{8,9},{9,8},{10,11... | collective-permute-start | bytes 2359304 | tf_op jit(solution)/shard_map/ppermute | solution.py:217
  343.0 14.6 %collective-permute-start.16 = (f32[5,384]{1,0:T(8,128)S(1)}, f32[5,384]{1,0:T(8,128)S(1)}, u32[]{:S(2)}, u32[]{:S(2)}) collective-permute-start(f32[5,384]{1,0:T(8,128)S(1)} %pad_maximum_fusion.17), channel_id=1, source_target_pairs={{0,2},{2,0},{1,3},{3,1},{4,6},{6,4},{5,7},{7,5},{8,10},{10,8},{9,1... | collective-permute-start | bytes 23048 | tf_op jit(solution)/shard_map/ppermute | solution.py:220
  392.9 69.6 %copy-start.35 = (f32[384]{0:T(512)}, f32[384]{0:T(512)S(1)}, u32[]{:S(2)}) copy-start(f32[384]{0:T(512)S(1)} %get-tuple-element.225) | copy-start | bytes 4612
  (42 other events, 337.4 us)
Sparse Core Ops, SparseCore 0:
  314.9 140.2 all-reduce.2

commit v2 on v1

--- a/solution.py
+++ b/solution.py
@@ -9,32 +9,24 @@
 
 HEAD_DIM = 64
 ROT = 16
+LANES = 128
 
 
 norm_epsilon = 1e-05
 masked_fill = -1e30
 
 
-def rotary_tables(position):
-    steps = jnp.arange(ROT // 2, dtype=jnp.int32).astype(jnp.float32)
+def lane_tables(position):
+    lane = jnp.arange(LANES, dtype=jnp.int32)
+    steps = (lane % (ROT // 2)).astype(jnp.float32)
     inverse = 10000.0 ** (-2.0 * steps / ROT)
     angle = position.astype(jnp.float32)[:, None] * inverse[None, :]
-    angle = jnp.concatenate([angle, angle], axis=1)
-    return (jnp.cos(angle), jnp.sin(angle))
-
-
-def rotary(part, cosines, sines):
-    turned = part[..., :ROT]
-    swapped = jnp.concatenate([-turned[..., ROT // 2 :], turned[..., : ROT // 2]], axis=-1)
-    rotated = turned * cosines[:, None, :] + swapped * sines[:, None, :]
-    return jnp.concatenate([rotated, part[..., ROT:]], axis=-1)
-
-
-def rotary_back(grads, cosines, sines):
-    turned = grads[..., :ROT]
-    scaled = turned * sines[:, None, :]
-    swapped = jnp.concatenate([scaled[..., ROT // 2 :], -scaled[..., : ROT // 2]], axis=-1)
-    return jnp.concatenate([turned * cosines[:, None, :] + swapped, grads[..., ROT:]], axis=-1)
+    sines = jnp.sin(angle)
+    return (
+        jnp.where(lane < ROT, jnp.cos(angle), 1.0),
+        jnp.where(lane < ROT // 2, -sines, 0.0),
+        jnp.where((lane >= ROT // 2) & (lane < ROT), sines, 0.0),
+    )
 
 
 def gelu_exact(values):
@@ -46,21 +38,36 @@
 
 
 def attention_kernel(
-    block, low_ref, seg_col, seg_row, q_ref, k_ref, v_ref, do_ref, ctx_ref, dq_ref, dk_ref, dv_ref
+    block, low_ref, seg_col, seg_row, joined_ref, do_ref, cos_ref, up_ref, down_ref,
+    ctx_ref, dj_ref, q_ref, k_ref, v_ref, dk_ref, dv_ref,
 ):
     heads, length, depth = q_ref.shape
     nt = (((1,), (1,)), ((), ()))
     tn = (((0,), (0,)), ((), ()))
-    dk_ref[...] = jnp.zeros_like(dk_ref)
-    dv_ref[...] = jnp.zeros_like(dv_ref)
+
+    def place(h, part):
+        return slice((3 * h + part) * depth, (3 * h + part + 1) * depth)
+
+    def turn(u, rows, sign):
+        up = pltpu.roll(u, depth - ROT // 2, 1) * up_ref[rows, :]
+        down = pltpu.roll(u, ROT // 2, 1) * down_ref[rows, :]
+        return u * cos_ref[rows, :] + sign * (up + down)
 
     def query_step(i, carry):
         rows = pl.ds(pl.multiple_of(i * block, block), block)
         low = low_ref[i]
         segs = seg_col[rows, :]
         places = i * block + lax.broadcasted_iota(jnp.int32, (block, block), 0)
+        for h in range(heads):
+            q_ref[h, rows, :] = turn(joined_ref[rows, place(h, 0)], rows, 1.0).astype(
+                jnp.bfloat16
+            ) * jnp.bfloat16(HEAD_DIM ** (-0.5))
+            k_ref[h, rows, :] = turn(joined_ref[rows, place(h, 1)], rows, 1.0).astype(jnp.bfloat16)
+            v_ref[h, rows, :] = joined_ref[rows, place(h, 2)].astype(jnp.bfloat16)
+            dk_ref[h, rows, :] = jnp.zeros((block, depth), jnp.float32)
+            dv_ref[h, rows, :] = jnp.zeros((block, depth), jnp.float32)
         queries = [q_ref[h, rows, :] for h in range(heads)]
-        grads = [do_ref[h, rows, :] for h in range(heads)]
+        grads = [do_ref[rows, h * depth : (h + 1) * depth] for h in range(heads)]
 
         def masked_scores(j, cols):
             key_places = j * block + lax.broadcasted_iota(jnp.int32, (block, block), 1)
@@ -110,7 +117,7 @@
         for h in range(heads):
             highest, total, acc = state[h]
             context = acc / total
-            ctx_ref[h, rows, :] = context.astype(jnp.bfloat16)
+            ctx_ref[rows, h * depth : (h + 1) * depth] = context.astype(jnp.bfloat16)
             lse.append(highest + jnp.log(total))
             inner.append(
                 jnp.sum(context * grads[h].astype(jnp.float32), axis=1, keepdims=True)
@@ -145,40 +152,66 @@
             tuple(jnp.zeros((block, depth), jnp.float32) for _ in range(heads)),
         )
         for h in range(heads):
-            dq_ref[h, rows, :] = state[h] * HEAD_DIM ** (-0.5)
+            dj_ref[rows, place(h, 0)] = turn(
+                state[h] * HEAD_DIM ** (-0.5), rows, -1.0
+            ).astype(jnp.bfloat16)
         return carry
 
     lax.fori_loop(0, length // block, query_step, 0)
 
-
-def attention(queries, keys, values, grads, segments):
-    heads, length, depth = queries.shape
+    def key_step(j, carry):
+        rows = pl.ds(pl.multiple_of(j * block, block), block)
+        for h in range(heads):
+            dj_ref[rows, place(h, 1)] = turn(dk_ref[h, rows, :], rows, -1.0).astype(jnp.bfloat16)
+            dj_ref[rows, place(h, 2)] = dv_ref[h, rows, :].astype(jnp.bfloat16)
+        return carry
+
+    lax.fori_loop(0, length // block, key_step, 0)
+
+
+def attention(joined, grads, tables, segments):
+    length = joined.shape[0]
+    heads = grads.shape[1] // LANES
     block = min(BLOCK, length)
     count = length // block
     firsts = segments.reshape(count, block)[:, 0]
     low = jnp.sum((segments[None, :] < firsts[:, None]).astype(jnp.int32), axis=1) // block
     vmem = pl.BlockSpec(memory_space=pltpu.VMEM)
-    wide = jax.ShapeDtypeStruct((heads, length, depth), jnp.float32)
+    held = (heads, length, LANES)
     return pl.pallas_call(
         functools.partial(attention_kernel, block),
-        out_shape=(jax.ShapeDtypeStruct((heads, length, depth), jnp.bfloat16), wide, wide, wide),
-        in_specs=[pl.BlockSpec(memory_space=pltpu.SMEM)] + [vmem] * 6,
-        out_specs=(vmem,) * 4,
+        out_shape=(
+            jax.ShapeDtypeStruct((length, heads * LANES), jnp.bfloat16),
+            jax.ShapeDtypeStruct((length, 3 * heads * LANES), jnp.bfloat16),
+        ),
+        in_specs=[pl.BlockSpec(memory_space=pltpu.SMEM)] + [vmem] * 7,
+        out_specs=(vmem,) * 2,
+        scratch_shapes=[pltpu.VMEM(held, jnp.bfloat16)] * 3 + [pltpu.VMEM(held, jnp.float32)] * 2,
         compiler_params=pltpu.CompilerParams(vmem_limit_bytes=48 * 1024 * 1024),
         cost_estimate=pl.CostEstimate(
-            flops=7 * 2 * heads * length * length // 4 * depth,
-            bytes_accessed=heads * length * depth * 22,
+            flops=7 * 2 * heads * length * length // 4 * LANES,
+            bytes_accessed=joined.size * 8,
             transcendentals=heads * length * length // 2,
         ),
     )(
         low,
         segments[:, None],
         segments.reshape(count, 1, block),
-        queries,
-        keys,
-        values,
+        joined,
         grads,
-    )
+        *tables,
+    )
+
+
+def pack_total(part):
+    size = lax.axis_size("dp")
+    if size & (size - 1):
+        return lax.psum(part, "dp")
+    step = 1
+    while step < size:
+        part = part + lax.ppermute(part, "dp", [(i, i ^ step) for i in range(size)])
+        step *= 2
+    return part
 
 
 def in_order(index, mine, other, axis=0):
@@ -225,23 +258,55 @@
         other = lax.dynamic_slice_in_dim(array, (1 - col) * half, half, axis)
         return mine, other
 
-    def whole_rows(part):
-        wide = jnp.concatenate([part, swap_col(part)], axis=1)
+    def whole_rows(part, part_other):
+        wide = jnp.concatenate([part, part_other], axis=1)
         return in_order(row, wide, swap_row(wide))
 
-    x_all = whole_rows(tokens)
+    def tn_dot(left, right):
+        return lax.dot_general(left, right, (((0,), (0,)), ((), ())), preferred_element_type=f32)
+
+    def nt_dot(left, right):
+        return lax.dot_general(left, right, (((1,), (1,)), ((), ())), preferred_element_type=f32)
+
+    hold = lax.optimization_barrier
     norms = jnp.stack([gain_one, shift_one, gain_two, shift_two])
-    norms = jnp.concatenate([norms, swap_col(norms)], axis=1)
-
+    norms_other = swap_col(norms)
+    norms = jnp.concatenate([norms, norms_other], axis=1)
+    tokens_other = swap_col(tokens)
+    in_mine, in_other = split_half(w_in, 1)
+    out_mine, out_other = split_half(w_out, 0)
     qkv_mine, qkv_other = split_half(w_qkv, 1)
+    dense_mine, dense_other = split_half(w_dense, 0)
+    tokens_other, in_other, cotangent_late = hold((tokens_other, in_other, cotangent))
+    x_all = whole_rows(tokens, tokens_other)
+    in_other = swap_col(in_other)
+    cotangent_other = swap_col(cotangent_late)
+    in_other, out_other, qkv_other, dense_other = hold(
+        (in_other, out_other, qkv_other, dense_other)
+    )
+    in_w = jnp.concatenate([in_mine, in_other], axis=0)
+    out_w = jnp.concatenate([out_mine, swap_col(out_other)], axis=1)
+    g_all = whole_rows(cotangent, cotangent_other)
     qkv_w = jnp.concatenate([qkv_mine, swap_col(qkv_other)], axis=0)
-    g_all = whole_rows(cotangent)
-    dense_mine, dense_other = split_half(w_dense, 0)
     dense_w = jnp.concatenate([dense_mine, swap_col(dense_other)], axis=1)
-    in_mine, in_other = split_half(w_in, 1)
-    in_w = jnp.concatenate([in_mine, swap_col(in_other)], axis=0)
-    out_mine, out_other = split_half(w_out, 0)
-    out_w = jnp.concatenate([out_mine, swap_col(out_other)], axis=1)
+
+    qkv_half = qkv_w.shape[1]
+    heads = qkv_half // (3 * HEAD_DIM)
+    parts = 3 * heads
+    narrow = jnp.arange(qkv_half, dtype=jnp.int32)
+    spread_out = (
+        (narrow // HEAD_DIM * LANES + narrow % HEAD_DIM)[:, None]
+        == jnp.arange(parts * LANES, dtype=jnp.int32)[None, :]
+    ).astype(bf16)
+    qkv_wide = jnp.dot(qkv_w, spread_out, preferred_element_type=f32).astype(bf16)
+    gap = LANES - HEAD_DIM
+    qkv_bias = jnp.pad(
+        split_half(b_qkv, 0)[0].reshape(parts, HEAD_DIM), ((0, 0), (0, gap))
+    ).reshape(-1)
+    dense_wide = jnp.pad(
+        dense_w.reshape(heads, HEAD_DIM, features), ((0, 0), (0, gap), (0, 0))
+    ).reshape(heads * LANES, features)
+    tables = lane_tables(positions)
 
     inputs = x_all.astype(f32)
     average = jnp.mean(inputs, axis=1, keepdims=True)
@@ -251,29 +316,17 @@
     first_in = (normed * norms[0] + norms[1]).astype(bf16)
     second_in = (normed * norms[2] + norms[3]).astype(bf16)
 
-    joined = jnp.dot(first_in, qkv_w, preferred_element_type=f32) + split_half(b_qkv, 0)[0]
-    joined = joined.reshape(length, -1, 3, HEAD_DIM)
-    cosines, sines = rotary_tables(positions)
-    query_heads = jnp.transpose(
-        (rotary(joined[:, :, 0], cosines, sines)).astype(bf16) * bf16(HEAD_DIM ** (-0.5)),
-        (1, 0, 2),
-    )
-    key_heads = jnp.transpose(rotary(joined[:, :, 1], cosines, sines).astype(bf16), (1, 0, 2))
-    value_heads = jnp.transpose(joined[:, :, 2].astype(bf16), (1, 0, 2))
-    d_context = jnp.dot(g_all, dense_w.T, preferred_element_type=f32).astype(bf16)
-    grad_heads = jnp.transpose(d_context.reshape(length, -1, HEAD_DIM), (1, 0, 2))
-    contexts, query_grads, key_grads, value_grads = attention(
-        query_heads, key_heads, value_heads, grad_heads, segments
-    )
-    context = jnp.transpose(contexts, (1, 0, 2)).reshape(length, -1)
-
     hidden = jnp.dot(second_in, in_w, preferred_element_type=f32) + split_half(b_in, 0)[0]
     active = gelu_exact(hidden).astype(bf16)
-    d_active = jnp.dot(g_all, out_w.T, preferred_element_type=f32)
+    d_active = nt_dot(g_all, out_w)
     d_hidden = jax.vjp(gelu_exact, hidden)[1](d_active)[0].astype(bf16)
-
-    def tn_dot(left, right):
-        return lax.dot_general(left, right, (((0,), (0,)), ((), ())), preferred_element_type=f32)
+    d_out = tn_dot(active, g_all).astype(bf16)
+    d_in = tn_dot(second_in, d_hidden).astype(bf16)
+
+    first_in, d_out, d_in, g_late = hold((first_in, d_out, d_in, g_all))
+    joined = jnp.dot(first_in, qkv_wide, preferred_element_type=f32) + qkv_bias
+    d_context = nt_dot(g_late, dense_wide).astype(bf16)
+    context, d_joined = attention(joined, d_context, tables, segments)
 
     def own_rows(partial):
         mine = lax.dynamic_slice_in_dim(partial, row * rows_here, rows_here, 0)
@@ -283,36 +336,31 @@
     def own_block(summed):
         return summed[:, :width] + swap_col(summed[:, width:].astype(bf16)).astype(f32)
 
-    def pack_sum(mine, other, axis):
-        both = in_order(col, mine.astype(bf16), swap_col(other.astype(bf16)), axis)
-        return lax.psum(both, "dp").astype(f32)
-
-    d_out = tn_dot(active, g_all)
-    d_out = pack_sum(d_out[:, :width], d_out[:, width:], 0)
-    d_in = tn_dot(second_in, d_hidden)
-    d_in = pack_sum(d_in[:width], d_in[width:], 1)
-    d_dense = tn_dot(context, g_all)
-    d_dense = pack_sum(d_dense[:, :width], d_dense[:, width:], 0)
-
-    query_back = rotary_back(jnp.transpose(query_grads, (1, 0, 2)), cosines, sines)
-    key_back = rotary_back(jnp.transpose(key_grads, (1, 0, 2)), cosines, sines)
-    value_back = jnp.transpose(value_grads, (1, 0, 2))
-    d_joined = (
-        jnp.stack([query_back, key_back, value_back], axis=2).reshape(length, -1).astype(bf16)
-    )
-    d_qkv = tn_dot(first_in, d_joined)
-    d_qkv = pack_sum(d_qkv[:width], d_qkv[width:], 1)
+    def pair(mine, other, axis):
+        return in_order(col, mine, swap_col(other), axis)
+
+    d_out, d_in = lax.psum(
+        (pair(d_out[:, :width], d_out[:, width:], 0), pair(d_in[:width], d_in[width:], 1)), "dp"
+    )
+    d_dense = tn_dot(context, g_all).astype(bf16)
+    d_dense = d_dense.reshape(heads, LANES, features)[:, :HEAD_DIM].reshape(-1, features)
+    d_qkv = nt_dot(tn_dot(first_in, d_joined).astype(bf16), spread_out).astype(bf16)
+    d_dense = pair(d_dense[:, :width], d_dense[:, width:], 0)
+    d_qkv = pair(d_qkv[:width], d_qkv[width:], 1)
+    d_out, d_in, d_dense, d_qkv = hold((d_out, d_in, d_dense, d_qkv))
+    d_dense, d_qkv = lax.psum((d_dense, d_qkv), "dp")
+    d_out, d_in, d_dense, d_qkv = (part.astype(f32) for part in (d_out, d_in, d_dense, d_qkv))
 
     branches = own_block(
         own_rows(
-            jnp.dot(context, dense_w, preferred_element_type=f32)
+            jnp.dot(context, dense_wide, preferred_element_type=f32)
             + jnp.dot(active, out_w, preferred_element_type=f32)
         )
     )
     mixed = tokens.astype(f32) + branches + b_dense + b_out
 
-    d_first = lax.dot_general(d_joined, qkv_w, (((1,), (1,)), ((), ())), preferred_element_type=f32)
-    d_second = lax.dot_general(d_hidden, in_w, (((1,), (1,)), ((), ())), preferred_element_type=f32)
+    d_first = nt_dot(d_joined, qkv_wide)
+    d_second = nt_dot(d_hidden, in_w)
     hat = own_rows(d_first * norms[0] + d_second * norms[2])
     own_inputs = lax.dynamic_slice_in_dim(x_all, row * rows_here, rows_here, 0).astype(f32)
     own_average = lax.dynamic_slice_in_dim(average, row * rows_here, rows_here, 0)
@@ -338,15 +386,18 @@
     vectors = jnp.concatenate([vectors, jnp.sum(cotangent, axis=0, dtype=f32)[None]], axis=0)
     vectors = vectors + swap_row(vectors)
     biases = jnp.concatenate(
-        [jnp.sum(d_joined, axis=0, dtype=f32), jnp.sum(d_hidden, axis=0, dtype=f32)]
+        [
+            jnp.sum(d_joined, axis=0, dtype=f32).reshape(parts, LANES)[:, :HEAD_DIM].reshape(-1),
+            jnp.sum(d_hidden, axis=0, dtype=f32),
+        ]
     )
     other_biases = swap_col(biases)
-    small = lax.psum(jnp.concatenate([vectors.reshape(-1), biases, other_biases]), "dp")
+    small = pack_total(jnp.concatenate([vectors.reshape(-1), biases, other_biases]))
     vectors = small[: 5 * width].reshape(5, width)
     total = biases.shape[0]
     own_bias = small[5 * width : 5 * width + total]
     other_bias = small[5 * width + total :]
-    cut = d_joined.shape[1]
+    cut = qkv_half
     d_qkv_bias = in_order(col, own_bias[:cut], other_bias[:cut])
     d_in_bias = in_order(col, own_bias[cut:], other_bias[cut:])
     return (

time: 475 us -> 477 us (level)
  waiting for transfers between devices: 134 us -> 207 us
  local copies, waits for them, and re-layouts: 77.2 us -> 30.3 us
  blocking collectives: 34.6 us -> 0 us
  other arithmetic: 58.6 us -> 38.3 us
  starting transfers between devices: 20.2 us -> 40.5 us
  matrix products: 71.4 us -> 83.6 us
  Pallas kernels: 59.5 us -> 54.4 us
    psum x1 -> x2, waiting for transfers between devices: 60.8 us -> 132 us  [the longest x1 74.9 us: body(): d_dense, d_qkv = lax.psum((d_dense, d_qkv), 'dp')]
    psum x1 -> x0, blocking collectives: 34.6 us -> none  [body(): lax.psum(jnp.concatenate([vectors.reshape(-1), biases, other_biases]), 'dp')]
    dot_general x6 -> x8, matrix products: 31.4 us -> 51.2 us  [the longest x5 40 us: nt_dot(): lax.dot_general(left, right, (((1,), (1,)), ((), ())), preferred_element_...]
    ppermute x0 -> x3, starting transfers between devices: none -> 17.6 us  [pack_total(): part = part + lax.ppermute(part, 'dp', [(i, i ^ step) for i in range(size)])]
    neg x2 -> x0, other arithmetic: 13 us -> none  [rotary(): -turned[..., ROT // 2:]]
    slice x13 -> x6, local copies, waits for them, and re-layouts: 15 us -> 3.24 us  [the longest x1 1.36 us: body(): d_out[:, :width]]
    unnamed x96 -> x80, local copies, waits for them, and re-layouts: 21.4 us -> 11 us
    another operation x3 -> x0, other arithmetic: 7.33 us -> none
  transfers between devices with their start and end apart: 22 -> 26, of which waited for: 8 -> 9; matrix products, arithmetic and copies ran while one was open for 35% -> 19% of each run, Pallas kernels for 13% -> 0%
where the time goes in v2:
time: 477 us; the launch traced here: 469 us
  waiting for transfers between devices  207 us (43%)
  matrix products  83.6 us (18%)
  Pallas kernels  54.4 us (11%)
  starting transfers between devices  40.5 us (8%)
  other arithmetic  38.3 us (8%)
  local copies, waits for them, and re-layouts  30.3 us (6%)
  between operations  15.2 us (3%)
    psum x1, waiting for transfers between devices, body(): d_dense, d_qkv = lax.psum((d_dense, d_qkv), 'dp')  74.9 us
    ppermute x16, waiting for transfers between devices, swap_col(): return lax.ppermute(part, 'col', SWAP)  74.4 us
    psum x1, waiting for transfers between devices, body(): lax.psum((pair(d_out[:, :width], d_out[:, width:], 0), pair(d_in[:width],...  57.5 us
    pallas_call x1, Pallas kernels, attention(): pl.pallas_call(functools.partial(attention_kernel, block), out_shape=(jax...  54.4 us
    dot_general x5, matrix products, nt_dot(): lax.dot_general(left, right, (((1,), (1,)), ((), ())), preferred_element_...  40 us
    ppermute x16, starting transfers between devices, swap_col(): return lax.ppermute(part, 'col', SWAP)  22.3 us
    dot_general x1, matrix products, body(): jnp.dot(second_in, in_w, preferred_element_type=f32)  20.5 us
    ppermute x3, starting transfers between devices, pack_total(): part = part + lax.ppermute(part, 'dp', [(i, i ^ step) for i in range(size)])  17.6 us
  transfers between devices with their start and end apart: 26, of which 9 were waited for; matrix products, arithmetic and copies ran while one was open for 19% of the time, Pallas kernels for 0%

profile of v2, /device:TPU:0, one launch (start us, length us, event | category | flops | bytes accessed | tf_op | source)
XLA Modules:
  0.0 469.2 jit_solution(10159366703444860175)
XLA Ops:
  7.3 3.0 collective-permute-start
  18.7 5.8 %fusion.25 = (f32[2048,128]{1,0:T(8,128)}, f32[2048,128]{1,0:T(8,128)}, f32[2048,128]{1,0:T(8,128)}) fusion(f32[128]{0:T(128)S(1)} %fusion.49, f32[2048]{0:T(1024)S(1)} %convert_element_type.113, pred[128]{0:T(512)(128)(4,1)S(1)} %get-tuple-element.165, pred[128]{0:T(512)(128)(4,1)S(1)} %get-tuple-element.166, pred[128]{0:T(512)(128)(4,1)S(1)} %iota_compare_fusion.6), kind=kLoop, calls=%fused_computation.67 | loop fusion | flops 1310720 | bytes 3154816 | tf_op jit(solution)/shard_map/jit(_where)/select_n | solution.py:28
  24.5 3.8 collective-permute-done
  35.6 12.8 %collective-permute-done.3 = bf16[384,768]{1,0:T(8,128)(2,1)} collective-permute-done((bf16[384,768]{1,0:T(8,128)(2,1)}, bf16[384,768]{1,0:T(8,128)(2,1)}, u32[]{:S(2)}, u32[]{:S(2)}) %collective-permute-start.3) | collective-permute-done | bytes 589856 | tf_op jit(solution)/shard_map/ppermute | solution.py:250
  52.3 26.6 %collective-permute-done.8 = bf16[192,384]{1,0:T(8,128)(2,1)S(1)} collective-permute-done((bf16[192,384]{1,0:T(8,128)(2,1)}, bf16[192,384]{1,0:T(8,128)(2,1)S(1)}, u32[]{:S(2)}, u32[]{:S(2)}) %collective-permute-start.8) | collective-permute-done | bytes 147488 | tf_op jit(solution)/shard_map/ppermute | solution.py:250
  84.3 3.7 convert_reduce_fusion
  88.1 20.5 %multiply_convert_fusion = (bf16[2048,768]{1,0:T(8,128)(2,1)S(1)}, f32[2048,768]{1,0:T(8,128)}, f32[2048,768]{1,0:T(8,128)}) fusion(f32[768]{0:T(1024)S(1)} %dynamic_slice.54, bf16[384,768]{1,0:T(8,128)(2,1)} %collective-permute-done.3, bf16[384,768]{1,0:T(8,128)(2,1)S(1)} %copy-done.25, bf16[2048,768]{1,0:T(8,128)(2,1)S(1)} %get-tuple-element.125, ...), kind=kOutput, calls=%fused_computation.22 | convolution fusion | flops 2531524608 | bytes 20079616 | tf_op jit(solution)/shard_map/dot_general | solution.py:319
  111.4 9.6 %convert_reduce_fusion.2 = (f32[768]{0:T(1024)S(1)}, bf16[2048,768]{1,0:T(8,128)(2,1)S(1)}) fusion(f32[2048,768]{1,0:T(8,128)} %get-tuple-element.124, bf16[2048,768]{1,0:T(8,128)(2,1)S(1)} %maximum_select_fusion.1, bf16[768,384]{1,0:T(8,128)(2,1)S(1)} %collective-permute-done.6, bf16[768,384]{1,0:T(8,128)(2,1)S(1)} %copy-done.23, ...), kind=kOutput, calls=%fused_computation.19 | convolution fusion | flops 2445016320 | bytes 20060160 | tf_op jit(solution)/shard_map/dot_general | solution.py:269
  121.1 4.2 convolution_convert_fusion.3
  125.3 3.7 convolution_convert_fusion.4
  131.9 6.6 %convolution_add_fusion.joined_ref = f32[2048,1152]{1,0:T(8,128)} fusion(bf16[2048,768]{1,0:T(8,128)(2,1)S(1)} %fusion.6, bf16[768,1152]{1,0:T(8,128)(2,1)S(1)} %convolution_convert_fusion, f32[1152]{0:T(1024)S(1)} %pad_bitcast_fusion), kind=kOutput, calls=%fused_computation.5 | convolution fusion | flops 3626237952 | bytes 14356992 | tf_op jit(solution)/shard_map/dot_general | solution.py:327
  138.6 54.4 %shard_map.263 = (bf16[2048,384]{1,0:T(8,128)(2,1)S(1)}, bf16[2048,1152]{1,0:T(8,128)(2,1)}) custom-call(s32[8]{0:T(128)S(1)} %and_select_fusion.1.low_ref, s32[2048,1]{1,0:T(8,128)S(1)} %copy.35.seg_col, s32[8,1,256]{2,1,0:T(1,128)S(1)} %bitcast.33, f32[2048,1152]{1,0:T(8,128)} %convolution_add_fusion.joined_ref, ...), custom_call_target="tpu_custom_call" | custom-call | flops 5637144576 | bytes 18874368 | tf_op jit(solution)/shard_map/pallas_call | solution.py:181
  192.9 8.6 %fusion.69 = f32[2048,768]{1,0:T(8,128)} fusion(bf16[2048,1152]{1,0:T(8,128)(2,1)} %get-tuple-element.41, bf16[768,1152]{1,0:T(8,128)(2,1)S(1)} %convolution_convert_fusion), kind=kOutput, calls=%fused_computation.159 | convolution fusion | flops 3623878656 | bytes 12779520 | tf_op jit(solution)/shard_map/dot_general | solution.py:269
  202.2 11.5 %fusion.27 = bf16[768,576]{0,1:T(8,128)(2,1)} fusion(s32[576]{0:T(1024)S(1)} %fusion.45, bf16[2048,768]{1,0:T(8,128)(2,1)} %copy-done.13, bf16[2048,1152]{1,0:T(8,128)(2,1)} %get-tuple-element.41), kind=kOutput, calls=%fused_computation.69 | convolution fusion | flops 4645085184 | bytes 8751360 | tf_op jit(solution)/shard_map/dot_general | solution.py:269
  213.7 7.3 %fusion.9 = (f32[768]{0:T(1024)S(1)}, f32[768]{0:T(1024)S(1)}, f32[768]{0:T(1024)S(1)}, f32[768]{0:T(1024)S(1)}, f32[2048,768]{1,0:T(8,128)S(1)}) fusion(f32[2048,768]{1,0:T(8,128)} %fusion.69, bf16[2048,768]{1,0:T(8,128)(2,1)} %copy-done.4, f32[2048]{0:T(1024)S(1)} %get-tuple-element.161, f32[2048]{0:T(1024)S(1)} %get-tuple-element.160, ...), kind=kOutput, calls=%fused_computation.15 | convolution fusion | flops 2437149696 | bytes 20088832 | tf_op jit(solution)/shard_map/dot_general | solution.py:269
  246.3 9.4 %collective-permute-done.15 = bf16[384,768]{1,0:T(8,128)(2,1)S(1)} collective-permute-done((bf16[384,768]{1,0:T(8,128)(2,1)S(1)}, bf16[384,768]{1,0:T(8,128)(2,1)S(1)}, u32[]{:S(2)}, u32[]{:S(2)}) %collective-permute-start.15) | collective-permute-done | bytes 589856 | tf_op jit(solution)/shard_map/ppermute | solution.py:250
  257.1 3.6 fusion.58
  268.4 14.0 %collective-permute-done.13 = f32[2,1024]{1,0:T(2,128)S(1)} collective-permute-done((f32[2,1024]{1,0:T(2,128)S(1)}, f32[2,1024]{1,0:T(2,128)S(1)}, u32[]{:S(2)}, u32[]{:S(2)}) %collective-permute-start.13) | collective-permute-done | bytes 8224 | tf_op jit(solution)/shard_map/ppermute | solution.py:250
  287.0 7.3 %collective-permute-start.21 = (f32[4608]{0:T(1024)S(1)}, f32[4608]{0:T(1024)S(1)}, u32[]{:S(2)}, u32[]{:S(2)}) collective-permute-start(f32[4608]{0:T(1024)S(1)} %concatenate.100), channel_id=1, source_target_pairs={{0,4},{4,0},{8,12},{12,8},{16,20},{20,16},{24,28},{28,24},{1,5},{5... | collective-permute-start | bytes 55304 | tf_op jit(solution)/shard_map/ppermute | solution.py:212
  294.2 7.3 %collective-permute-done.16 = bf16[192,384]{1,0:T(8,128)(2,1)S(1)} collective-permute-done((bf16[192,384]{1,0:T(8,128)(2,1)}, bf16[192,384]{1,0:T(8,128)(2,1)S(1)}, u32[]{:S(2)}, u32[]{:S(2)}) %collective-permute-start.16) | collective-permute-done | bytes 147488 | tf_op jit(solution)/shard_map/ppermute | solution.py:250
  303.4 3.8 collective-permute-start.22
  309.8 6.5 %collective-permute-start.23 = (f32[4608]{0:T(1024)S(1)}, f32[4608]{0:T(1024)S(1)}, u32[]{:S(2)}, u32[]{:S(2)}) collective-permute-start(f32[4608]{0:T(1024)S(1)} %add.237), channel_id=1, source_target_pairs={{0,16},{4,20},{8,24},{12,28},{16,0},{20,4},{24,8},{28,12},{1,17},{... | collective-permute-start | bytes 55304 | tf_op jit(solution)/shard_map/ppermute | solution.py:212
  316.3 57.5 %all-reduce.9.cloned.1.call-done = (bf16[1536,384]{1,0:T(8,128)(2,1)}, bf16[384,1536]{1,0:T(8,128)(2,1)}) async-done(((bf16[1536,384]{1,0:T(8,128)(2,1)}, bf16[384,1536]{1,0:T(8,128)(2,1)}), (bf16[1536,384]{1,0:T(8,128)(2,1)}, bf16[384,1536]{1,0:T(8,128)(2,1)})) %all-reduce.9.cloned.1.call-update) | async-done | bytes 2359312 | tf_op jit(solution)/shard_map/psum | solution.py:342
  382.1 74.9 %all-reduce.7.cloned.1.call-done = (bf16[384,1152]{0,1:T(8,128)(2,1)}, bf16[384,384]{1,0:T(8,128)(2,1)}) async-done(((bf16[384,1152]{0,1:T(8,128)(2,1)}, bf16[384,384]{1,0:T(8,128)(2,1)}), (bf16[384,1152]{0,1:T(8,128)(2,1)}, bf16[384,384]{1,0:T(8,128)(2,1)})) %all-reduce.7.cloned.1.call-update) | async-done | bytes 1179664 | tf_op jit(solution)/shard_map/psum | solution.py:351
  (206 shorter events, 87.7 us)
Async XLA Ops:
  7.2 366.6 %all-reduce.9.cloned.1.call-start = ((), (), s32[]{:S(2)}) async-start(), calls=%async_computation.1 | async-start | bytes 4718592 | tf_op jit(solution)/shard_map/psum | solution.py:342
  7.3 21.0 %collective-permute-start = (bf16[1024,384]{1,0:T(8,128)(2,1)}, bf16[1024,384]{1,0:T(8,128)(2,1)}, u32[]{:S(2)}, u32[]{:S(2)}) collective-permute-start(bf16[1024,384]{1,0:T(8,128)(2,1)} %param.16), channel_id=1, source_target_pairs={{0,1},{1,0},{2,3},{3,2},{4,5},{5,4},{6,7},{7,6},{8,9},{9,8},{10,11... | collective-permute-start | bytes 2359304 | tf_op jit(solution)/shard_map/ppermute | solution.py:250
  13.1 37.4 %collective-permute-start.2 = (f32[4,384]{1,0:T(4,128)S(1)}, f32[4,384]{1,0:T(4,128)S(1)}, u32[]{:S(2)}, u32[]{:S(2)}) collective-permute-start(f32[4,384]{1,0:T(4,128)S(1)} %pad_maximum_fusion.14), channel_id=1, source_target_pairs={{0,1},{1,0},{2,3},{3,2},{4,5},{5,4},{6,7},{7,6},{8,9},{9,8},{10,11... | collective-permute-start | bytes 18440 | tf_op jit(solution)/shard_map/ppermute | solution.py:250
  30.3 53.9 %collective-permute-start.1 = (bf16[1024,768]{1,0:T(8,128)(2,1)}, bf16[1024,768]{1,0:T(8,128)(2,1)}, u32[]{:S(2)}, u32[]{:S(2)}) collective-permute-start(bf16[1024,768]{1,0:T(8,128)(2,1)} %constant_dynamic-update-slice_fusion), channel_id=1, source_target_pairs={{0,2},{2,0},{1,3},{3,1},{4,6},{6,4},{5,7},{7,5},{8,10},{10,8},{9,1... | collective-permute-start | bytes 4718600 | tf_op jit(solution)/shard_map/ppermute | solution.py:253
  31.9 16.4 %collective-permute-start.3 = (bf16[384,768]{1,0:T(8,128)(2,1)}, bf16[384,768]{1,0:T(8,128)(2,1)}, u32[]{:S(2)}, u32[]{:S(2)}) collective-permute-start(bf16[384,768]{1,0:T(8,128)(2,1)} %get-tuple-element.32), channel_id=1, source_target_pairs={{0,1},{1,0},{2,3},{3,2},{4,5},{5,4},{6,7},{7,6},{8,9},{9,8},{10,11... | collective-permute-start | bytes 1769480 | tf_op jit(solution)/shard_map/ppermute | solution.py:250
  34.8 45.0 %collective-permute-start.4 = (bf16[1024,384]{1,0:T(8,128)(2,1)S(1)}, bf16[1024,384]{1,0:T(8,128)(2,1)}, u32[]{:S(2)}, u32[]{:S(2)}) collective-permute-start(bf16[1024,384]{1,0:T(8,128)(2,1)S(1)} %copy-done.9), channel_id=1, source_target_pairs={{0,1},{1,0},{2,3},{3,2},{4,5},{5,4},{6,7},{7,6},{8,9},{9,8},{10,11... | collective-permute-start | bytes 2359304 | tf_op jit(solution)/shard_map/ppermute | solution.py:250
  48.4 33.0 %collective-permute-start.7 = (bf16[384,576]{1,0:T(8,128)(2,1)}, bf16[384,576]{1,0:T(8,128)(2,1)S(1)}, u32[]{:S(2)}, u32[]{:S(2)}) collective-permute-start(bf16[384,576]{1,0:T(8,128)(2,1)} %get-tuple-element.37), channel_id=1, source_target_pairs={{0,1},{1,0},{2,3},{3,2},{4,5},{5,4},{6,7},{7,6},{8,9},{9,8},{10,11... | collective-permute-start | bytes 1327112 | tf_op jit(solution)/shard_map/ppermute | solution.py:250
  50.1 28.7 %collective-permute-start.8 = (bf16[192,384]{1,0:T(8,128)(2,1)}, bf16[192,384]{1,0:T(8,128)(2,1)S(1)}, u32[]{:S(2)}, u32[]{:S(2)}) collective-permute-start(bf16[192,384]{1,0:T(8,128)(2,1)} %get-tuple-element.39), channel_id=1, source_target_pairs={{0,1},{1,0},{2,3},{3,2},{4,5},{5,4},{6,7},{7,6},{8,9},{9,8},{10,11... | collective-permute-start | bytes 442376 | tf_op jit(solution)/shard_map/ppermute | solution.py:250
  50.5 60.4 %collective-permute-start.6 = (bf16[768,384]{1,0:T(8,128)(2,1)}, bf16[768,384]{1,0:T(8,128)(2,1)S(1)}, u32[]{:S(2)}, u32[]{:S(2)}) collective-permute-start(bf16[768,384]{1,0:T(8,128)(2,1)} %get-tuple-element.35), channel_id=1, source_target_pairs={{0,1},{1,0},{2,3},{3,2},{4,5},{5,4},{6,7},{7,6},{8,9},{9,8},{10,11... | collective-permute-start | bytes 1769480 | tf_op jit(solution)/shard_map/ppermute | solution.py:250
  81.3 28.6 %collective-permute-start.5 = (bf16[1024,768]{1,0:T(8,128)(2,1)S(1)}, bf16[1024,768]{1,0:T(8,128)(2,1)S(1)}, u32[]{:S(2)}, u32[]{:S(2)}) collective-permute-start(bf16[1024,768]{1,0:T(8,128)(2,1)S(1)} %constant_dynamic-update-slice_fusion.2), channel_id=1, source_target_pairs={{0,2},{2,0},{1,3},{3,1},{4,6},{6,4},{5,7},{7,5},{8,10},{10,8},{9,1... | collective-permute-start | bytes 4718600 | tf_op jit(solution)/shard_map/ppermute | solution.py:253
  221.1 19.6 %collective-permute-start.18 = (f32[4,384]{1,0:T(4,128)S(1)}, f32[4,384]{1,0:T(4,128)S(1)}, u32[]{:S(2)}, u32[]{:S(2)}) collective-permute-start(f32[4,384]{1,0:T(4,128)S(1)} %slice.172), channel_id=1, source_target_pairs={{0,1},{1,0},{2,3},{3,2},{4,5},{5,4},{6,7},{7,6},{8,9},{9,8},{10,11... | collective-permute-start | bytes 18440 | tf_op jit(solution)/shard_map/ppermute | solution.py:250
  224.9 32.2 %collective-permute-start.11 = (bf16[1024,768]{1,0:T(8,128)(2,1)}, bf16[1024,768]{1,0:T(8,128)(2,1)}, u32[]{:S(2)}, u32[]{:S(2)}) collective-permute-start(bf16[1024,768]{1,0:T(8,128)(2,1)} %dynamic-slice_convert_fusion), channel_id=1, source_target_pairs={{0,2},{2,0},{1,3},{3,1},{4,6},{6,4},{5,7},{7,5},{8,10},{10,8},{9,1... | collective-permute-start | bytes 4718600 | tf_op jit(solution)/shard_map/ppermute | solution.py:253
  226.8 16.2 %collective-permute-start.14 = (bf16[768,384]{1,0:T(8,128)(2,1)S(1)}, bf16[768,384]{1,0:T(8,128)(2,1)S(1)}, u32[]{:S(2)}, u32[]{:S(2)}) collective-permute-start(bf16[768,384]{1,0:T(8,128)(2,1)S(1)} %get-tuple-element.131), channel_id=1, source_target_pairs={{0,1},{1,0},{2,3},{3,2},{4,5},{5,4},{6,7},{7,6},{8,9},{9,8},{10,11... | collective-permute-start | bytes 1769480 | tf_op jit(solution)/shard_map/ppermute | solution.py:250
  228.7 27.0 %collective-permute-start.15 = (bf16[384,768]{1,0:T(8,128)(2,1)S(1)}, bf16[384,768]{1,0:T(8,128)(2,1)S(1)}, u32[]{:S(2)}, u32[]{:S(2)}) collective-permute-start(bf16[384,768]{1,0:T(8,128)(2,1)S(1)} %get-tuple-element.129), channel_id=1, source_target_pairs={{0,1},{1,0},{2,3},{3,2},{4,5},{5,4},{6,7},{7,6},{8,9},{9,8},{10,11... | collective-permute-start | bytes 1769480 | tf_op jit(solution)/shard_map/ppermute | solution.py:250
  235.3 27.7 %collective-permute-start.9 = (bf16[1024,768]{1,0:T(8,128)(2,1)}, bf16[1024,768]{1,0:T(8,128)(2,1)}, u32[]{:S(2)}, u32[]{:S(2)}) collective-permute-start(bf16[1024,768]{1,0:T(8,128)(2,1)} %dynamic-slice_convert_fusion.1), channel_id=1, source_target_pairs={{0,2},{2,0},{1,3},{3,1},{4,6},{6,4},{5,7},{7,5},{8,10},{10,8},{9,1... | collective-permute-start | bytes 4718600 | tf_op jit(solution)/shard_map/ppermute | solution.py:253
  240.8 46.1 %collective-permute-start.20 = (f32[1344]{0:T(1024)S(1)}, f32[1344]{0:T(1024)S(1)}, u32[]{:S(2)}, u32[]{:S(2)}) collective-permute-start(f32[1344]{0:T(1024)S(1)} %pad_maximum_fusion.13), channel_id=1, source_target_pairs={{0,1},{1,0},{2,3},{3,2},{4,5},{5,4},{6,7},{7,6},{8,9},{9,8},{10,11... | collective-permute-start | bytes 16136 | tf_op jit(solution)/shard_map/ppermute | solution.py:250
  243.1 64.1 %collective-permute-start.17 = (bf16[384,576]{0,1:T(8,128)(2,1)}, bf16[384,576]{0,1:T(8,128)(2,1)}, u32[]{:S(2)}, u32[]{:S(2)}) collective-permute-start(bf16[384,576]{0,1:T(8,128)(2,1)} %get-tuple-element.137), channel_id=1, source_target_pairs={{0,1},{1,0},{2,3},{3,2},{4,5},{5,4},{6,7},{7,6},{8,9},{9,8},{10,11... | collective-permute-start | bytes 1327112 | tf_op jit(solution)/shard_map/ppermute | solution.py:250
  257.0 200.0 %all-reduce.7.cloned.1.call-start = ((), (), s32[]{:S(2)}) async-start(), calls=%async_computation | async-start | bytes 2359296 | tf_op jit(solution)/shard_map/psum | solution.py:351
  260.8 21.6 %collective-permute-start.12 = (bf16[1024,384]{1,0:T(8,128)(2,1)S(1)}, bf16[1024,384]{1,0:T(8,128)(2,1)S(1)}, u32[]{:S(2)}, u32[]{:S(2)}) collective-permute-start(bf16[1024,384]{1,0:T(8,128)(2,1)S(1)} %slice.210), channel_id=1, source_target_pairs={{0,1},{1,0},{2,3},{3,2},{4,5},{5,4},{6,7},{7,6},{8,9},{9,8},{10,11... | collective-permute-start | bytes 2359304 | tf_op jit(solution)/shard_map/ppermute | solution.py:250
  262.7 19.7 %collective-permute-start.13 = (f32[2,1024]{1,0:T(2,128)S(1)}, f32[2,1024]{1,0:T(2,128)S(1)}, u32[]{:S(2)}, u32[]{:S(2)}) collective-permute-start(f32[2,1024]{1,0:T(2,128)S(1)} %pad_maximum_fusion.12), channel_id=1, source_target_pairs={{0,1},{1,0},{2,3},{3,2},{4,5},{5,4},{6,7},{7,6},{8,9},{9,8},{10,11... | collective-permute-start | bytes 24584 | tf_op jit(solution)/shard_map/ppermute | solution.py:250
  266.6 107.2 %collective-permute-start.10 = (bf16[1024,384]{1,0:T(8,128)(2,1)}, bf16[1024,384]{1,0:T(8,128)(2,1)}, u32[]{:S(2)}, u32[]{:S(2)}) collective-permute-start(bf16[1024,384]{1,0:T(8,128)(2,1)} %slice.211), channel_id=1, source_target_pairs={{0,1},{1,0},{2,3},{3,2},{4,5},{5,4},{6,7},{7,6},{8,9},{9,8},{10,11... | collective-permute-start | bytes 2359304 | tf_op jit(solution)/shard_map/ppermute | solution.py:250
  285.1 16.5 %collective-permute-start.16 = (bf16[192,384]{1,0:T(8,128)(2,1)}, bf16[192,384]{1,0:T(8,128)(2,1)S(1)}, u32[]{:S(2)}, u32[]{:S(2)}) collective-permute-start(bf16[192,384]{1,0:T(8,128)(2,1)} %get-tuple-element.143), channel_id=1, source_target_pairs={{0,1},{1,0},{2,3},{3,2},{4,5},{5,4},{6,7},{7,6},{8,9},{9,8},{10,11... | collective-permute-start | bytes 442376 | tf_op jit(solution)/shard_map/ppermute | solution.py:250
  287.0 16.4 %collective-permute-start.21 = (f32[4608]{0:T(1024)S(1)}, f32[4608]{0:T(1024)S(1)}, u32[]{:S(2)}, u32[]{:S(2)}) collective-permute-start(f32[4608]{0:T(1024)S(1)} %concatenate.100), channel_id=1, source_target_pairs={{0,4},{4,0},{8,12},{12,8},{16,20},{20,16},{24,28},{28,24},{1,5},{5... | collective-permute-start | bytes 55304 | tf_op jit(solution)/shard_map/ppermute | solution.py:212
  309.8 67.1 %collective-permute-start.23 = (f32[4608]{0:T(1024)S(1)}, f32[4608]{0:T(1024)S(1)}, u32[]{:S(2)}, u32[]{:S(2)}) collective-permute-start(f32[4608]{0:T(1024)S(1)} %add.237), channel_id=1, source_target_pairs={{0,16},{4,20},{8,24},{12,28},{16,0},{20,4},{24,8},{28,12},{1,17},{... | collective-permute-start | bytes 55304 | tf_op jit(solution)/shard_map/ppermute | solution.py:212
  (40 other events, 635.2 us)
Sparse Core Ops, SparseCore 0:
  257.2 116.5 all-reduce.8
  377.7 79.3 all-reduce.6

commit v3 on v2

--- a/solution.py
+++ b/solution.py
@@ -326,6 +326,13 @@
     first_in, d_out, d_in, g_late = hold((first_in, d_out, d_in, g_all))
     joined = jnp.dot(first_in, qkv_wide, preferred_element_type=f32) + qkv_bias
     d_context = nt_dot(g_late, dense_wide).astype(bf16)
+    def pair(mine, other, axis):
+        return in_order(col, mine, swap_col(other), axis)
+
+    d_out = pair(d_out[:, :width], d_out[:, width:], 0)
+    d_in = pair(d_in[:width], d_in[width:], 1)
+    joined, d_context, d_out, d_in = hold((joined, d_context, d_out, d_in))
+    d_out, d_in = lax.psum((d_out, d_in), "dp")
     context, d_joined = attention(joined, d_context, tables, segments)
 
     def own_rows(partial):
@@ -336,12 +343,6 @@
     def own_block(summed):
         return summed[:, :width] + swap_col(summed[:, width:].astype(bf16)).astype(f32)
 
-    def pair(mine, other, axis):
-        return in_order(col, mine, swap_col(other), axis)
-
-    d_out, d_in = lax.psum(
-        (pair(d_out[:, :width], d_out[:, width:], 0), pair(d_in[:width], d_in[width:], 1)), "dp"
-    )
     d_dense = tn_dot(context, g_all).astype(bf16)
     d_dense = d_dense.reshape(heads, LANES, features)[:, :HEAD_DIM].reshape(-1, features)
     d_qkv = nt_dot(tn_dot(first_in, d_joined).astype(bf16), spread_out).astype(bf16)

time: 477 us -> 489 us (1.025); the launches traced: 469 us -> 488 us
  waiting for transfers between devices: 207 us -> 219 us
  starting transfers between devices: 40.5 us -> 46.4 us
    psum x1, waiting for transfers between devices: 57.5 us -> 67.7 us  [body(): d_out, d_in = lax.psum((d_out, d_in), 'dp')]
    ppermute x3, starting transfers between devices: 17.6 us -> 26.4 us  [pack_total(): part = part + lax.ppermute(part, 'dp', [(i, i ^ step) for i in range(size)])]
    unnamed x80 -> x82, local copies, waits for them, and re-layouts: 11 us -> 11.1 us
  transfers between devices with their start and end apart: 26 -> 26, of which waited for: 9 -> 8; matrix products, arithmetic and copies ran while one was open for 19% -> 20% of each run, Pallas kernels for 0% -> 0%
where the time goes in v3:
time: 489 us; the launch traced here: 488 us
  waiting for transfers between devices  219 us (45%)
  matrix products  83.3 us (17%)
  Pallas kernels  54.4 us (11%)
  starting transfers between devices  46.4 us (9%)
  other arithmetic  38.7 us (8%)
  local copies, waits for them, and re-layouts  31.1 us (6%)
  between operations  15.2 us (3%)
    ppermute x16, waiting for transfers between devices, swap_col(): return lax.ppermute(part, 'col', SWAP)  77 us
    psum x1, waiting for transfers between devices, body(): d_dense, d_qkv = lax.psum((d_dense, d_qkv), 'dp')  74.1 us
    psum x1, waiting for transfers between devices, body(): d_out, d_in = lax.psum((d_out, d_in), 'dp')  67.7 us
    pallas_call x1, Pallas kernels, attention(): pl.pallas_call(functools.partial(attention_kernel, block), out_shape=(jax...  54.4 us
    dot_general x5, matrix products, nt_dot(): lax.dot_general(left, right, (((1,), (1,)), ((), ())), preferred_element_...  39.8 us
    ppermute x3, starting transfers between devices, pack_total(): part = part + lax.ppermute(part, 'dp', [(i, i ^ step) for i in range(size)])  26.4 us
    dot_general x1, matrix products, body(): jnp.dot(second_in, in_w, preferred_element_type=f32)  20.5 us
    ppermute x16, starting transfers between devices, swap_col(): return lax.ppermute(part, 'col', SWAP)  19.2 us
  transfers between devices with their start and end apart: 26, of which 8 were waited for; matrix products, arithmetic and copies ran while one was open for 20% of the time, Pallas kernels for 0%

profile of v3, /device:TPU:0, one launch (start us, length us, event | category | flops | bytes accessed | tf_op | source)
XLA Modules:
  0.0 488.0 jit_solution(10449911504044667569)
XLA Ops:
  7.3 3.0 collective-permute-start
  18.7 5.7 %fusion.25 = (f32[2048,128]{1,0:T(8,128)}, f32[2048,128]{1,0:T(8,128)}, f32[2048,128]{1,0:T(8,128)}) fusion(f32[128]{0:T(128)S(1)} %fusion.49, f32[2048]{0:T(1024)S(1)} %convert_element_type.113, pred[128]{0:T(512)(128)(4,1)S(1)} %get-tuple-element.173, pred[128]{0:T(512)(128)(4,1)S(1)} %get-tuple-element.174, pred[128]{0:T(512)(128)(4,1)S(1)} %iota_compare_fusion.6), kind=kLoop, calls=%fused_computation.67 | loop fusion | flops 1310720 | bytes 3154816 | tf_op jit(solution)/shard_map/jit(_where)/select_n | solution.py:28
  24.4 3.8 collective-permute-done
  35.6 12.8 %collective-permute-done.3 = bf16[384,768]{1,0:T(8,128)(2,1)} collective-permute-done((bf16[384,768]{1,0:T(8,128)(2,1)}, bf16[384,768]{1,0:T(8,128)(2,1)}, u32[]{:S(2)}, u32[]{:S(2)}) %collective-permute-start.3) | collective-permute-done | bytes 589856 | tf_op jit(solution)/shard_map/ppermute | solution.py:250
  52.3 26.6 %collective-permute-done.8 = bf16[192,384]{1,0:T(8,128)(2,1)S(1)} collective-permute-done((bf16[192,384]{1,0:T(8,128)(2,1)}, bf16[192,384]{1,0:T(8,128)(2,1)S(1)}, u32[]{:S(2)}, u32[]{:S(2)}) %collective-permute-start.8) | collective-permute-done | bytes 147488 | tf_op jit(solution)/shard_map/ppermute | solution.py:250
  84.3 4.3 convert_reduce_fusion
  88.6 20.5 %multiply_convert_fusion = (bf16[2048,768]{1,0:T(8,128)(2,1)S(1)}, f32[2048,768]{1,0:T(8,128)}, f32[2048,768]{1,0:T(8,128)}) fusion(f32[768]{0:T(1024)S(1)} %dynamic_slice.54, bf16[384,768]{1,0:T(8,128)(2,1)} %collective-permute-done.3, bf16[384,768]{1,0:T(8,128)(2,1)S(1)} %copy-done.21, bf16[2048,768]{1,0:T(8,128)(2,1)S(1)} %get-tuple-element.133, ...), kind=kOutput, calls=%fused_computation.22 | convolution fusion | flops 2531524608 | bytes 20079616 | tf_op jit(solution)/shard_map/dot_general | solution.py:319
  112.0 9.6 %convert_reduce_fusion.2 = (f32[768]{0:T(1024)S(1)}, bf16[2048,768]{1,0:T(8,128)(2,1)S(1)}) fusion(f32[2048,768]{1,0:T(8,128)} %get-tuple-element.132, bf16[2048,768]{1,0:T(8,128)(2,1)S(1)} %maximum_select_fusion.1, bf16[768,384]{1,0:T(8,128)(2,1)S(1)} %collective-permute-done.6, bf16[768,384]{1,0:T(8,128)(2,1)S(1)} %copy-done.20, ...), kind=kOutput, calls=%fused_computation.19 | convolution fusion | flops 2445016320 | bytes 20060160 | tf_op jit(solution)/shard_map/dot_general | solution.py:269
  121.6 3.1 convolution_convert_fusion.3
  129.8 6.6 %convolution_add_fusion.joined_ref = f32[2048,1152]{1,0:T(8,128)} fusion(bf16[2048,768]{1,0:T(8,128)(2,1)S(1)} %fusion.6, bf16[768,1152]{1,0:T(8,128)(2,1)S(1)} %convolution_convert_fusion, f32[1152]{0:T(1024)S(1)} %pad_bitcast_fusion), kind=kOutput, calls=%fused_computation.5 | convolution fusion | flops 3626237952 | bytes 14356992 | tf_op jit(solution)/shard_map/dot_general | solution.py:327
  136.4 3.0 convolution_convert_fusion.2.do_ref
  139.4 4.3 collective-permute-done.10
  145.1 10.9 %collective-permute-done.9 = bf16[768,384]{1,0:T(8,128)(2,1)S(1)} collective-permute-done((bf16[768,384]{1,0:T(8,128)(2,1)S(1)}, bf16[768,384]{1,0:T(8,128)(2,1)S(1)}, u32[]{:S(2)}, u32[]{:S(2)}) %collective-permute-start.9) | collective-permute-done | bytes 589856 | tf_op jit(solution)/shard_map/ppermute | solution.py:250
  161.1 54.4 %shard_map.263 = (bf16[2048,384]{1,0:T(8,128)(2,1)S(1)}, bf16[2048,1152]{1,0:T(8,128)(2,1)}) custom-call(s32[8]{0:T(128)S(1)} %and_select_fusion.1.low_ref, s32[2048,1]{1,0:T(8,128)S(1)} %copy.35.seg_col, s32[8,1,256]{2,1,0:T(1,128)S(1)} %bitcast.33, f32[2048,1152]{1,0:T(8,128)} %convolution_add_fusion.joined_ref, ...), custom_call_target="tpu_custom_call" | custom-call | flops 5637144576 | bytes 18874368 | tf_op jit(solution)/shard_map/pallas_call | solution.py:181
  215.5 8.4 %fusion.69 = f32[2048,768]{1,0:T(8,128)} fusion(bf16[2048,1152]{1,0:T(8,128)(2,1)} %get-tuple-element.49, bf16[768,1152]{1,0:T(8,128)(2,1)S(1)} %copy-done.35), kind=kOutput, calls=%fused_computation.159 | convolution fusion | flops 3623878656 | bytes 12779520 | tf_op jit(solution)/shard_map/dot_general | solution.py:269
  223.9 11.5 %fusion.27 = bf16[768,576]{0,1:T(8,128)(2,1)} fusion(s32[576]{0:T(1024)S(1)} %fusion.45, bf16[2048,768]{1,0:T(8,128)(2,1)} %copy-done.11, bf16[2048,1152]{1,0:T(8,128)(2,1)} %get-tuple-element.49), kind=kOutput, calls=%fused_computation.69 | convolution fusion | flops 4645085184 | bytes 8751360 | tf_op jit(solution)/shard_map/dot_general | solution.py:269
  235.5 7.2 %fusion.9 = (f32[768]{0:T(1024)S(1)}, f32[768]{0:T(1024)S(1)}, f32[768]{0:T(1024)S(1)}, f32[768]{0:T(1024)S(1)}, f32[2048,768]{1,0:T(8,128)S(1)}) fusion(f32[2048,768]{1,0:T(8,128)} %fusion.69, bf16[2048,768]{1,0:T(8,128)(2,1)} %copy-done.4, f32[2048]{0:T(1024)S(1)} %get-tuple-element.169, f32[2048]{0:T(1024)S(1)} %get-tuple-element.168, ...), kind=kOutput, calls=%fused_computation.15 | convolution fusion | flops 2437149696 | bytes 20088832 | tf_op jit(solution)/shard_map/dot_general | solution.py:269
  248.0 4.5 convolution_add_fusion.1
  253.3 3.3 dynamic-slice_convert_fusion.1
  262.0 3.6 fusion.58
  272.5 18.6 %collective-permute-done.15 = f32[2,1024]{1,0:T(2,128)S(1)} collective-permute-done((f32[2,1024]{1,0:T(2,128)S(1)}, f32[2,1024]{1,0:T(2,128)S(1)}, u32[]{:S(2)}, u32[]{:S(2)}) %collective-permute-start.15) | collective-permute-done | bytes 8224 | tf_op jit(solution)/shard_map/ppermute | solution.py:250
  294.9 24.9 %collective-permute-start.21 = (f32[4608]{0:T(1024)S(1)}, f32[4608]{0:T(1024)S(1)}, u32[]{:S(2)}, u32[]{:S(2)}) collective-permute-start(f32[4608]{0:T(1024)S(1)} %concatenate.100), channel_id=1, source_target_pairs={{0,4},{4,0},{8,12},{12,8},{16,20},{20,16},{24,28},{28,24},{1,5},{5... | collective-permute-start | bytes 55304 | tf_op jit(solution)/shard_map/ppermute | solution.py:212
  324.2 67.7 %all-reduce.9.cloned.1.call-done = (bf16[1536,384]{1,0:T(8,128)(2,1)}, bf16[384,1536]{1,0:T(8,128)(2,1)}) async-done(((bf16[1536,384]{1,0:T(8,128)(2,1)}, bf16[384,1536]{1,0:T(8,128)(2,1)}), (bf16[1536,384]{1,0:T(8,128)(2,1)}, bf16[384,1536]{1,0:T(8,128)(2,1)})) %all-reduce.9.cloned.1.call-update) | async-done | bytes 2359312 | tf_op jit(solution)/shard_map/psum | solution.py:335
  401.7 74.1 %all-reduce.7.cloned.1.call-done = (bf16[384,1152]{0,1:T(8,128)(2,1)}, bf16[384,384]{1,0:T(8,128)(2,1)}) async-done(((bf16[384,1152]{0,1:T(8,128)(2,1)}, bf16[384,384]{1,0:T(8,128)(2,1)}), (bf16[384,1152]{0,1:T(8,128)(2,1)}, bf16[384,384]{1,0:T(8,128)(2,1)})) %all-reduce.7.cloned.1.call-update) | async-done | bytes 1179664 | tf_op jit(solution)/shard_map/psum | solution.py:352
  (209 shorter events, 80.2 us)
Async XLA Ops:
  7.2 384.8 %all-reduce.9.cloned.1.call-start = ((), (), s32[]{:S(2)}) async-start(), calls=%async_computation.1 | async-start | bytes 4718592 | tf_op jit(solution)/shard_map/psum | solution.py:335
  7.3 21.0 %collective-permute-start = (bf16[1024,384]{1,0:T(8,128)(2,1)}, bf16[1024,384]{1,0:T(8,128)(2,1)}, u32[]{:S(2)}, u32[]{:S(2)}) collective-permute-start(bf16[1024,384]{1,0:T(8,128)(2,1)} %param.16), channel_id=1, source_target_pairs={{0,1},{1,0},{2,3},{3,2},{4,5},{5,4},{6,7},{7,6},{8,9},{9,8},{10,11... | collective-permute-start | bytes 2359304 | tf_op jit(solution)/shard_map/ppermute | solution.py:250
  13.1 37.3 %collective-permute-start.2 = (f32[4,384]{1,0:T(4,128)S(1)}, f32[4,384]{1,0:T(4,128)S(1)}, u32[]{:S(2)}, u32[]{:S(2)}) collective-permute-start(f32[4,384]{1,0:T(4,128)S(1)} %pad_maximum_fusion.14), channel_id=1, source_target_pairs={{0,1},{1,0},{2,3},{3,2},{4,5},{5,4},{6,7},{7,6},{8,9},{9,8},{10,11... | collective-permute-start | bytes 18440 | tf_op jit(solution)/shard_map/ppermute | solution.py:250
  30.3 53.9 %collective-permute-start.1 = (bf16[1024,768]{1,0:T(8,128)(2,1)}, bf16[1024,768]{1,0:T(8,128)(2,1)}, u32[]{:S(2)}, u32[]{:S(2)}) collective-permute-start(bf16[1024,768]{1,0:T(8,128)(2,1)} %constant_dynamic-update-slice_fusion), channel_id=1, source_target_pairs={{0,2},{2,0},{1,3},{3,1},{4,6},{6,4},{5,7},{7,5},{8,10},{10,8},{9,1... | collective-permute-start | bytes 4718600 | tf_op jit(solution)/shard_map/ppermute | solution.py:253
  31.9 16.4 %collective-permute-start.3 = (bf16[384,768]{1,0:T(8,128)(2,1)}, bf16[384,768]{1,0:T(8,128)(2,1)}, u32[]{:S(2)}, u32[]{:S(2)}) collective-permute-start(bf16[384,768]{1,0:T(8,128)(2,1)} %get-tuple-element.36), channel_id=1, source_target_pairs={{0,1},{1,0},{2,3},{3,2},{4,5},{5,4},{6,7},{7,6},{8,9},{9,8},{10,11... | collective-permute-start | bytes 1769480 | tf_op jit(solution)/shard_map/ppermute | solution.py:250
  34.8 45.0 %collective-permute-start.4 = (bf16[1024,384]{1,0:T(8,128)(2,1)S(1)}, bf16[1024,384]{1,0:T(8,128)(2,1)}, u32[]{:S(2)}, u32[]{:S(2)}) collective-permute-start(bf16[1024,384]{1,0:T(8,128)(2,1)S(1)} %copy-done.7), channel_id=1, source_target_pairs={{0,1},{1,0},{2,3},{3,2},{4,5},{5,4},{6,7},{7,6},{8,9},{9,8},{10,11... | collective-permute-start | bytes 2359304 | tf_op jit(solution)/shard_map/ppermute | solution.py:250
  48.4 33.0 %collective-permute-start.7 = (bf16[384,576]{1,0:T(8,128)(2,1)}, bf16[384,576]{1,0:T(8,128)(2,1)S(1)}, u32[]{:S(2)}, u32[]{:S(2)}) collective-permute-start(bf16[384,576]{1,0:T(8,128)(2,1)} %get-tuple-element.41), channel_id=1, source_target_pairs={{0,1},{1,0},{2,3},{3,2},{4,5},{5,4},{6,7},{7,6},{8,9},{9,8},{10,11... | collective-permute-start | bytes 1327112 | tf_op jit(solution)/shard_map/ppermute | solution.py:250
  50.1 28.7 %collective-permute-start.8 = (bf16[192,384]{1,0:T(8,128)(2,1)}, bf16[192,384]{1,0:T(8,128)(2,1)S(1)}, u32[]{:S(2)}, u32[]{:S(2)}) collective-permute-start(bf16[192,384]{1,0:T(8,128)(2,1)} %get-tuple-element.43), channel_id=1, source_target_pairs={{0,1},{1,0},{2,3},{3,2},{4,5},{5,4},{6,7},{7,6},{8,9},{9,8},{10,11... | collective-permute-start | bytes 442376 | tf_op jit(solution)/shard_map/ppermute | solution.py:250
  50.5 61.0 %collective-permute-start.6 = (bf16[768,384]{1,0:T(8,128)(2,1)}, bf16[768,384]{1,0:T(8,128)(2,1)S(1)}, u32[]{:S(2)}, u32[]{:S(2)}) collective-permute-start(bf16[768,384]{1,0:T(8,128)(2,1)} %get-tuple-element.39), channel_id=1, source_target_pairs={{0,1},{1,0},{2,3},{3,2},{4,5},{5,4},{6,7},{7,6},{8,9},{9,8},{10,11... | collective-permute-start | bytes 1769480 | tf_op jit(solution)/shard_map/ppermute | solution.py:250
  81.3 29.1 %collective-permute-start.5 = (bf16[1024,768]{1,0:T(8,128)(2,1)S(1)}, bf16[1024,768]{1,0:T(8,128)(2,1)S(1)}, u32[]{:S(2)}, u32[]{:S(2)}) collective-permute-start(bf16[1024,768]{1,0:T(8,128)(2,1)S(1)} %constant_dynamic-update-slice_fusion.2), channel_id=1, source_target_pairs={{0,2},{2,0},{1,3},{3,1},{4,6},{6,4},{5,7},{7,5},{8,10},{10,8},{9,1... | collective-permute-start | bytes 4718600 | tf_op jit(solution)/shard_map/ppermute | solution.py:253
  127.6 16.2 %collective-permute-start.10 = (bf16[384,768]{1,0:T(8,128)(2,1)S(1)}, bf16[384,768]{1,0:T(8,128)(2,1)S(1)}, u32[]{:S(2)}, u32[]{:S(2)}) collective-permute-start(bf16[384,768]{1,0:T(8,128)(2,1)S(1)} %get-tuple-element.137), channel_id=1, source_target_pairs={{0,1},{1,0},{2,3},{3,2},{4,5},{5,4},{6,7},{7,6},{8,9},{9,8},{10,11... | collective-permute-start | bytes 1769480 | tf_op jit(solution)/shard_map/ppermute | solution.py:250
  129.5 26.5 %collective-permute-start.9 = (bf16[768,384]{1,0:T(8,128)(2,1)S(1)}, bf16[768,384]{1,0:T(8,128)(2,1)S(1)}, u32[]{:S(2)}, u32[]{:S(2)}) collective-permute-start(bf16[768,384]{1,0:T(8,128)(2,1)S(1)} %get-tuple-element.139), channel_id=1, source_target_pairs={{0,1},{1,0},{2,3},{3,2},{4,5},{5,4},{6,7},{7,6},{8,9},{9,8},{10,11... | collective-permute-start | bytes 1769480 | tf_op jit(solution)/shard_map/ppermute | solution.py:250
  242.8 19.0 %collective-permute-start.18 = (f32[4,384]{1,0:T(4,128)S(1)}, f32[4,384]{1,0:T(4,128)S(1)}, u32[]{:S(2)}, u32[]{:S(2)}) collective-permute-start(f32[4,384]{1,0:T(4,128)S(1)} %slice.172), channel_id=1, source_target_pairs={{0,1},{1,0},{2,3},{3,2},{4,5},{5,4},{6,7},{7,6},{8,9},{9,8},{10,11... | collective-permute-start | bytes 18440 | tf_op jit(solution)/shard_map/ppermute | solution.py:250
  245.9 16.0 %collective-permute-start.13 = (bf16[1024,768]{1,0:T(8,128)(2,1)}, bf16[1024,768]{1,0:T(8,128)(2,1)}, u32[]{:S(2)}, u32[]{:S(2)}) collective-permute-start(bf16[1024,768]{1,0:T(8,128)(2,1)} %dynamic-slice_convert_fusion), channel_id=1, source_target_pairs={{0,2},{2,0},{1,3},{3,1},{4,6},{6,4},{5,7},{7,5},{8,10},{10,8},{9,1... | collective-permute-start | bytes 4718600 | tf_op jit(solution)/shard_map/ppermute | solution.py:253
  256.7 11.2 %collective-permute-start.11 = (bf16[1024,768]{1,0:T(8,128)(2,1)}, bf16[1024,768]{1,0:T(8,128)(2,1)}, u32[]{:S(2)}, u32[]{:S(2)}) collective-permute-start(bf16[1024,768]{1,0:T(8,128)(2,1)} %dynamic-slice_convert_fusion.1), channel_id=1, source_target_pairs={{0,2},{2,0},{1,3},{3,1},{4,6},{6,4},{5,7},{7,5},{8,10},{10,8},{9,1... | collective-permute-start | bytes 4718600 | tf_op jit(solution)/shard_map/ppermute | solution.py:253
  257.2 37.5 %collective-permute-start.20 = (f32[1344]{0:T(1024)S(1)}, f32[1344]{0:T(1024)S(1)}, u32[]{:S(2)}, u32[]{:S(2)}) collective-permute-start(f32[1344]{0:T(1024)S(1)} %pad_maximum_fusion.13), channel_id=1, source_target_pairs={{0,1},{1,0},{2,3},{3,2},{4,5},{5,4},{6,7},{7,6},{8,9},{9,8},{10,11... | collective-permute-start | bytes 16136 | tf_op jit(solution)/shard_map/ppermute | solution.py:250
  260.8 60.8 %collective-permute-start.17 = (bf16[384,576]{0,1:T(8,128)(2,1)}, bf16[384,576]{0,1:T(8,128)(2,1)}, u32[]{:S(2)}, u32[]{:S(2)}) collective-permute-start(bf16[384,576]{0,1:T(8,128)(2,1)} %get-tuple-element.145), channel_id=1, source_target_pairs={{0,1},{1,0},{2,3},{3,2},{4,5},{5,4},{6,7},{7,6},{8,9},{9,8},{10,11... | collective-permute-start | bytes 1327112 | tf_op jit(solution)/shard_map/ppermute | solution.py:250
  261.8 214.1 %all-reduce.7.cloned.1.call-start = ((), (), s32[]{:S(2)}) async-start(), calls=%async_computation | async-start | bytes 2359296 | tf_op jit(solution)/shard_map/psum | solution.py:352
  265.7 25.4 %collective-permute-start.14 = (bf16[1024,384]{1,0:T(8,128)(2,1)S(1)}, bf16[1024,384]{1,0:T(8,128)(2,1)S(1)}, u32[]{:S(2)}, u32[]{:S(2)}) collective-permute-start(bf16[1024,384]{1,0:T(8,128)(2,1)S(1)} %slice.210), channel_id=1, source_target_pairs={{0,1},{1,0},{2,3},{3,2},{4,5},{5,4},{6,7},{7,6},{8,9},{9,8},{10,11... | collective-permute-start | bytes 2359304 | tf_op jit(solution)/shard_map/ppermute | solution.py:250
  266.8 24.3 %collective-permute-start.15 = (f32[2,1024]{1,0:T(2,128)S(1)}, f32[2,1024]{1,0:T(2,128)S(1)}, u32[]{:S(2)}, u32[]{:S(2)}) collective-permute-start(f32[2,1024]{1,0:T(2,128)S(1)} %pad_maximum_fusion.12), channel_id=1, source_target_pairs={{0,1},{1,0},{2,3},{3,2},{4,5},{5,4},{6,7},{7,6},{8,9},{9,8},{10,11... | collective-permute-start | bytes 24584 | tf_op jit(solution)/shard_map/ppermute | solution.py:250
  271.5 122.0 %collective-permute-start.12 = (bf16[1024,384]{1,0:T(8,128)(2,1)}, bf16[1024,384]{1,0:T(8,128)(2,1)}, u32[]{:S(2)}, u32[]{:S(2)}) collective-permute-start(bf16[1024,384]{1,0:T(8,128)(2,1)} %slice.211), channel_id=1, source_target_pairs={{0,1},{1,0},{2,3},{3,2},{4,5},{5,4},{6,7},{7,6},{8,9},{9,8},{10,11... | collective-permute-start | bytes 2359304 | tf_op jit(solution)/shard_map/ppermute | solution.py:250
  293.7 26.0 %collective-permute-start.16 = (bf16[192,384]{1,0:T(8,128)(2,1)}, bf16[192,384]{1,0:T(8,128)(2,1)S(1)}, u32[]{:S(2)}, u32[]{:S(2)}) collective-permute-start(bf16[192,384]{1,0:T(8,128)(2,1)} %get-tuple-element.151), channel_id=1, source_target_pairs={{0,1},{1,0},{2,3},{3,2},{4,5},{5,4},{6,7},{7,6},{8,9},{9,8},{10,11... | collective-permute-start | bytes 442376 | tf_op jit(solution)/shard_map/ppermute | solution.py:250
  294.9 26.7 %collective-permute-start.21 = (f32[4608]{0:T(1024)S(1)}, f32[4608]{0:T(1024)S(1)}, u32[]{:S(2)}, u32[]{:S(2)}) collective-permute-start(f32[4608]{0:T(1024)S(1)} %concatenate.100), channel_id=1, source_target_pairs={{0,4},{4,0},{8,12},{12,8},{16,20},{20,16},{24,28},{28,24},{1,5},{5... | collective-permute-start | bytes 55304 | tf_op jit(solution)/shard_map/ppermute | solution.py:212
  321.5 70.5 %collective-permute-start.22 = (f32[4608]{0:T(1024)S(1)}, f32[4608]{0:T(1024)S(1)}, u32[]{:S(2)}, u32[]{:S(2)}) collective-permute-start(f32[4608]{0:T(1024)S(1)} %add.236), channel_id=1, source_target_pairs={{0,8},{4,12},{8,0},{12,4},{16,24},{20,28},{24,16},{28,20},{1,9},{5... | collective-permute-start | bytes 55304 | tf_op jit(solution)/shard_map/ppermute | solution.py:212
  (41 other events, 739.0 us)
Sparse Core Ops, SparseCore 0:
  261.9 130.0 all-reduce.8
  396.5 79.3 all-reduce.6
